TPU v7x, 512 devices: a whole 4x4x16 slice. The times are simulated.
512 devices in a mesh: grp: 16 (over x_hi, y, core), dev: 32 (over x_lo, z).
Axes of the slice: x: 4 (x_hi: 2, x_lo: 2; x = x_hi * 2 + x_lo), y: 4, z: 16, core: 2. Of those that a mesh axis runs over, the one named last changes fastest.
Arguments:
- states: bfloat16 [2, 512, 128, 4096], P(None, ('grp', 'dev')), may hold values from -64 to 64
- lengths: int32 [2, 512], replicated, may hold values from 32 to 128
Outputs:
- utility: float32 [2, 512], P(None, ('grp', 'dev'))
- best_match: float32 [2, 512, 128], P(None, ('grp', 'dev'))
All inputs are finite; a program needn't handle non-finite values.
Results may differ from a plain program's by a relative error of at most 0.00059.
Values may be sent and summed in bfloat16 or wider, within the bound.
No kernel may reach another device: no remote copies, remote signals or barrier semaphores. Data moves between devices by JAX's collectives and lax.ppermute only.
A program may use at most 64 MiB of HBM per device.

v0:
```python
import jax
import jax.numpy as jnp
from jax import lax
from jax.sharding import PartitionSpec as P

ROUNDS = 2


epsilon = 1e-06
sentinel = -4.0


def from_partner(value, axis, bit):
    mask = 2**bit
    pairs = [(source, source ^ mask) for source in range(lax.axis_size(axis))]
    return lax.ppermute(value, axis, pairs)


def passed_along(value, axis, by):
    count = lax.axis_size(axis)
    return lax.ppermute(value, axis, [(i, (i + by) % count) for i in range(count)])


def normalize(states):
    values = states.astype(jnp.float32)
    inverse_norm = lax.rsqrt(jnp.sum(values * values, axis=-1, keepdims=True) + epsilon)
    return (values * inverse_norm).astype(jnp.bfloat16)


def pick_prompt(block, prompt):
    return lax.dynamic_index_in_dim(block, prompt, 0, keepdims=False)


def table_entry(lengths, prompt, candidate):
    row_ids = jnp.arange(lengths.shape[0], dtype=jnp.int32)[:, None]
    column_ids = jnp.arange(lengths.shape[1], dtype=jnp.int32)[None, :]
    chosen = (row_ids == prompt) & (column_ids == candidate)
    return jnp.sum(jnp.where(chosen, lengths, 0))


def score_pair(own_block, other_block, own_len, other_len):
    similarity = jnp.einsum("td,ud->tu", own_block, other_block, preferred_element_type=jnp.float32)
    positions = jnp.arange(own_block.shape[0], dtype=jnp.int32)
    own_valid = positions < own_len
    other_valid = positions < other_len
    row_best = jnp.max(jnp.where(other_valid[None, :], similarity, sentinel), axis=1)
    column_best = jnp.max(jnp.where(own_valid[:, None], similarity, sentinel), axis=0)
    own_mean = jnp.sum(jnp.where(own_valid, row_best, 0.0)) / own_len.astype(jnp.float32)
    other_mean = jnp.sum(jnp.where(other_valid, column_best, 0.0)) / other_len.astype(jnp.float32)
    return (row_best, column_best, 0.5 * (own_mean + other_mean))


def body(states, lengths):
    prompts = states.shape[0]
    tokens = states.shape[2]
    unit_states = normalize(states[:, 0])
    devices = lax.axis_size("dev")
    group_index = lax.axis_index("grp")
    member = lax.axis_index("dev")
    own_cand = group_index * devices + member
    prompt_ids = jnp.arange(prompts, dtype=jnp.int32)
    column_ids = jnp.arange(lengths.shape[1], dtype=jnp.int32)[None, :]
    own_lengths = jnp.sum(jnp.where(column_ids == own_cand, lengths, 0), axis=1)
    utility = jnp.zeros((prompts,), jnp.float32)
    best_match = jnp.full((prompts, tokens), sentinel, jnp.float32)
    for round_index in range(ROUNDS):
        stride = 2**round_index
        upper_flag = group_index // stride % 2
        partner_group = group_index + stride - 2 * stride * upper_flag
        partner_block = from_partner(unit_states, "grp", round_index)
        blocks = [partner_block]
        current = partner_block
        for offset in range(1, 3):
            current = passed_along(current, "dev", -1)
            blocks.append(current)
        blocks.append(passed_along(pick_prompt(current, upper_flag), "dev", -1))
        slot_list = [
            (0, True, False),
            (1, True, True),
            (2, True, True),
            (3, True, True),
            (0, False, False),
            (1, False, True),
            (2, False, True),
        ]
        outgoing_max = [jnp.full((prompts, tokens), sentinel, jnp.float32) for offset in range(4)]
        outgoing_sum = [jnp.zeros((prompts,), jnp.float32) for offset in range(4)]
        for offset, leading, always in slot_list:
            prompt = upper_flag if leading else 1 - upper_flag
            own_block = pick_prompt(unit_states, prompt)
            other_block = blocks[3] if offset == 3 else pick_prompt(blocks[offset], prompt)
            other_cand = partner_group * devices + (member + offset) % devices
            own_len = jnp.sum(jnp.where(prompt_ids == prompt, own_lengths, 0))
            other_len = table_entry(lengths, prompt, other_cand)
            row_best, column_best, pair_score = score_pair(
                own_block, other_block, own_len, other_len
            )
            if not always:
                active = upper_flag == 0
                row_best = jnp.where(active, row_best, sentinel)
                column_best = jnp.where(active, column_best, sentinel)
                pair_score = jnp.where(active, pair_score, 0.0)
            prompt_mask = prompt_ids == prompt
            best_match = jnp.where(
                prompt_mask[:, None], jnp.maximum(best_match, row_best[None, :]), best_match
            )
            utility = utility + jnp.where(prompt_mask, pair_score, 0.0)
            outgoing_max[offset] = jnp.where(
                prompt_mask[:, None],
                jnp.maximum(outgoing_max[offset], column_best[None, :]),
                outgoing_max[offset],
            )
            outgoing_sum[offset] = outgoing_sum[offset] + jnp.where(prompt_mask, pair_score, 0.0)
        carry_max = outgoing_max[3]
        carry_sum = outgoing_sum[3]
        for offset in (2, 1, 0):
            moved_max, moved_sum = passed_along((carry_max, carry_sum), "dev", 1)
            carry_max = jnp.maximum(moved_max, outgoing_max[offset])
            carry_sum = moved_sum + outgoing_sum[offset]
        home_max, home_sum = from_partner((carry_max, carry_sum), "grp", round_index)
        best_match = jnp.maximum(best_match, home_max)
        utility = utility + home_sum
    token_valid = jnp.arange(tokens, dtype=jnp.int32)[None, :] < own_lengths[:, None]
    best_match = jnp.where(token_valid, best_match, 0.0)
    return (utility[:, None], best_match[:, None, :])


def solution(mesh):
    in_specs = (P(None, ("grp", "dev"), None, None), P())
    out_specs = (P(None, ("grp", "dev")), P(None, ("grp", "dev"), None))
    return jax.shard_map(body, mesh=mesh, in_specs=in_specs, out_specs=out_specs, check_vma=False)
```

profile of v0, /device:TPU:1, one launch (start us, length us, event | category | flops | bytes accessed | tf_op | source)
XLA Modules:
  0.0 358.3 jit_solution(14109988053834269935)
XLA Ops:
  0.6 2.2 fusion
  3.5 4.0 %collective-permute-start.8 = (bf16[2,128,4096]{2,1,0:T(8,128)(2,1)S(1)}, bf16[2,128,4096]{2,1,0:T(8,128)(2,1)}, u32[]{:S(2)}, u32[]{:S(2)}) collective-permute-start(bf16[2,128,4096]{2,1,0:T(8,128)(2,1)S(1)} %fusion.1), channel_id=1, source_target_pairs={{0,64},{32,96},{64,0},{96,32},{128,192},{160,224},{192,128},{224,1... | collective-permute-start | bytes 6291464 | tf_op jit(solution)/shard_map/ppermute | solution.py:16
  7.5 6.7 %collective-permute-start = (bf16[2,128,4096]{2,1,0:T(8,128)(2,1)S(1)}, bf16[2,128,4096]{2,1,0:T(8,128)(2,1)}, u32[]{:S(2)}, u32[]{:S(2)}) collective-permute-start(bf16[2,128,4096]{2,1,0:T(8,128)(2,1)S(1)} %fusion.1), channel_id=1, source_target_pairs={{0,32},{32,0},{64,96},{96,64},{128,160},{160,128},{192,224},{224,1... | collective-permute-start | bytes 6291464 | tf_op jit(solution)/shard_map/ppermute | solution.py:16
  14.2 33.7 %collective-permute-done.8 = bf16[2,128,4096]{2,1,0:T(8,128)(2,1)} collective-permute-done((bf16[2,128,4096]{2,1,0:T(8,128)(2,1)S(1)}, bf16[2,128,4096]{2,1,0:T(8,128)(2,1)}, u32[]{:S(2)}, u32[]{:S(2)}) %collective-permute-start.8) | collective-permute-done | bytes 2097184 | tf_op jit(solution)/shard_map/ppermute | solution.py:16
  47.9 16.9 %collective-permute-start.9 = (bf16[2,128,4096]{2,1,0:T(8,128)(2,1)}, bf16[2,128,4096]{2,1,0:T(8,128)(2,1)}, u32[]{:S(2)}, u32[]{:S(2)}) collective-permute-start(bf16[2,128,4096]{2,1,0:T(8,128)(2,1)} %collective-permute-done.8), channel_id=1, source_target_pairs={{0,31},{1,0},{2,1},{3,2},{4,3},{5,4},{6,5},{7,6},{8,7},{9,8},{10,9... | collective-permute-start | bytes 6291464 | tf_op jit(solution)/shard_map/ppermute | solution.py:21
  65.1 2.6 collective-permute-start.1
  82.4 26.1 %collective-permute-done.9 = bf16[2,128,4096]{2,1,0:T(8,128)(2,1)} collective-permute-done((bf16[2,128,4096]{2,1,0:T(8,128)(2,1)}, bf16[2,128,4096]{2,1,0:T(8,128)(2,1)}, u32[]{:S(2)}, u32[]{:S(2)}) %collective-permute-start.9) | collective-permute-done | bytes 2097184 | tf_op jit(solution)/shard_map/ppermute | solution.py:21
  108.5 6.2 %collective-permute-start.10 = (bf16[2,128,4096]{2,1,0:T(8,128)(2,1)}, bf16[2,128,4096]{2,1,0:T(8,128)(2,1)S(1)}, u32[]{:S(2)}, u32[]{:S(2)}) collective-permute-start(bf16[2,128,4096]{2,1,0:T(8,128)(2,1)} %collective-permute-done.9), channel_id=1, source_target_pairs={{0,31},{1,0},{2,1},{3,2},{4,3},{5,4},{6,5},{7,6},{8,7},{9,8},{10,9... | collective-permute-start | bytes 6291464 | tf_op jit(solution)/shard_map/ppermute | solution.py:21
  125.7 27.8 %collective-permute-done.1 = bf16[2,128,4096]{2,1,0:T(8,128)(2,1)} collective-permute-done((bf16[2,128,4096]{2,1,0:T(8,128)(2,1)}, bf16[2,128,4096]{2,1,0:T(8,128)(2,1)}, u32[]{:S(2)}, u32[]{:S(2)}) %collective-permute-start.1) | collective-permute-done | bytes 2097184 | tf_op jit(solution)/shard_map/ppermute | solution.py:21
  153.5 6.2 %collective-permute-start.2 = (bf16[2,128,4096]{2,1,0:T(8,128)(2,1)}, bf16[2,128,4096]{2,1,0:T(8,128)(2,1)}, u32[]{:S(2)}, u32[]{:S(2)}) collective-permute-start(bf16[2,128,4096]{2,1,0:T(8,128)(2,1)} %collective-permute-done.1), channel_id=1, source_target_pairs={{0,31},{1,0},{2,1},{3,2},{4,3},{5,4},{6,5},{7,6},{8,7},{9,8},{10,9... | collective-permute-start | bytes 6291464 | tf_op jit(solution)/shard_map/ppermute | solution.py:21
  171.4 27.0 %collective-permute-done.10 = bf16[2,128,4096]{2,1,0:T(8,128)(2,1)S(1)} collective-permute-done((bf16[2,128,4096]{2,1,0:T(8,128)(2,1)}, bf16[2,128,4096]{2,1,0:T(8,128)(2,1)S(1)}, u32[]{:S(2)}, u32[]{:S(2)}) %collective-permute-start.10) | collective-permute-done | bytes 2097184 | tf_op jit(solution)/shard_map/ppermute | solution.py:21
  209.5 2.3 dynamic-slice_bitcast_fusion
  211.9 6.1 %collective-permute-start.11 = (bf16[128,4096]{1,0:T(8,128)(2,1)}, bf16[128,4096]{1,0:T(8,128)(2,1)}, u32[]{:S(2)}, u32[]{:S(2)}) collective-permute-start(bf16[128,4096]{1,0:T(8,128)(2,1)} %dynamic-slice_bitcast_fusion), channel_id=1, source_target_pairs={{0,31},{1,0},{2,1},{3,2},{4,3},{5,4},{6,5},{7,6},{8,7},{9,8},{10,9... | collective-permute-start | bytes 3145736 | tf_op jit(solution)/shard_map/ppermute | solution.py:21
  218.0 25.4 %collective-permute-done.2 = bf16[2,128,4096]{2,1,0:T(8,128)(2,1)} collective-permute-done((bf16[2,128,4096]{2,1,0:T(8,128)(2,1)}, bf16[2,128,4096]{2,1,0:T(8,128)(2,1)}, u32[]{:S(2)}, u32[]{:S(2)}) %collective-permute-start.2) | collective-permute-done | bytes 2097184 | tf_op jit(solution)/shard_map/ppermute | solution.py:21
  254.5 2.5 dynamic-slice_bitcast_fusion.1
  257.0 6.2 %collective-permute-start.3 = (bf16[128,4096]{1,0:T(8,128)(2,1)}, bf16[128,4096]{1,0:T(8,128)(2,1)S(1)}, u32[]{:S(2)}, u32[]{:S(2)}) collective-permute-start(bf16[128,4096]{1,0:T(8,128)(2,1)} %dynamic-slice_bitcast_fusion.1), channel_id=1, source_target_pairs={{0,31},{1,0},{2,1},{3,2},{4,3},{5,4},{6,5},{7,6},{8,7},{9,8},{10,9... | collective-permute-start | bytes 3145736 | tf_op jit(solution)/shard_map/ppermute | solution.py:21
  263.2 2.6 collective-permute-done.11
  283.1 1.9 collective-permute-start.12
  305.7 1.9 collective-permute-start.4
  307.6 1.9 collective-permute-start.16
  309.6 2.5 collective-permute-start.13
  312.7 2.9 collective-permute-start.5
  316.6 3.8 %collective-permute-start.14 = (f32[2]{0:T(128)S(1)}, f32[2]{0:T(128)S(1)}, u32[]{:S(2)}, u32[]{:S(2)}) collective-permute-start(f32[2]{0:T(128)S(1)} %add_add_fusion.1), channel_id=1, source_target_pairs={{0,1},{1,2},{2,3},{3,4},{4,5},{5,6},{6,7},{7,8},{8,9},{9,10},{10,1... | collective-permute-start | bytes 32 | tf_op jit(solution)/shard_map/ppermute | solution.py:21
  320.4 3.2 collective-permute-start.6
  323.6 3.2 collective-permute-start.15
  326.9 9.1 %collective-permute-start.7 = (f32[2]{0:T(128)S(1)}, f32[2]{0:T(128)S(1)}, u32[]{:S(2)}, u32[]{:S(2)}) collective-permute-start(f32[2]{0:T(128)S(1)} %add_add_fusion.3), channel_id=1, source_target_pairs={{0,32},{32,0},{64,96},{96,64},{128,160},{160,128},{192,224},{224,1... | collective-permute-start | bytes 32 | tf_op jit(solution)/shard_map/ppermute | solution.py:16
  336.1 2.5 collective-permute-start.21
  338.7 3.4 collective-permute-start.17
  342.6 2.7 collective-permute-start.22
  345.3 2.9 collective-permute-start.18
  349.1 3.2 collective-permute-start.23
  352.4 4.5 %collective-permute-start.19 = (f32[2,128]{1,0:T(2,128)S(1)}, f32[2,128]{1,0:T(2,128)S(1)}, u32[]{:S(2)}, u32[]{:S(2)}) collective-permute-start(f32[2,128]{1,0:T(2,128)S(1)} %fusion.95), channel_id=1, source_target_pairs={{0,32},{32,0},{64,96},{96,64},{128,160},{160,128},{192,224},{224,1... | collective-permute-start | bytes 3080 | tf_op jit(solution)/shard_map/ppermute | solution.py:16
  (114 shorter events, 73.8 us)
Async XLA Ops:
  0.6 2.3 copy-start
  2.9 64.9 %copy-start.3 = (s32[2,512]{1,0:T(2,128)S(1)}, s32[2,512]{1,0:T(2,128)}, u32[]{:S(2)}) copy-start(s32[2,512]{1,0:T(2,128)} %param.3) | copy-start | bytes 12292
  3.5 44.5 %collective-permute-start.8 = (bf16[2,128,4096]{2,1,0:T(8,128)(2,1)S(1)}, bf16[2,128,4096]{2,1,0:T(8,128)(2,1)}, u32[]{:S(2)}, u32[]{:S(2)}) collective-permute-start(bf16[2,128,4096]{2,1,0:T(8,128)(2,1)S(1)} %fusion.1), channel_id=1, source_target_pairs={{0,64},{32,96},{64,0},{96,32},{128,192},{160,224},{192,128},{224,1... | collective-permute-start | bytes 6291464 | tf_op jit(solution)/shard_map/ppermute | solution.py:16
  7.5 57.6 %collective-permute-start = (bf16[2,128,4096]{2,1,0:T(8,128)(2,1)S(1)}, bf16[2,128,4096]{2,1,0:T(8,128)(2,1)}, u32[]{:S(2)}, u32[]{:S(2)}) collective-permute-start(bf16[2,128,4096]{2,1,0:T(8,128)(2,1)S(1)} %fusion.1), channel_id=1, source_target_pairs={{0,32},{32,0},{64,96},{96,64},{128,160},{160,128},{192,224},{224,1... | collective-permute-start | bytes 6291464 | tf_op jit(solution)/shard_map/ppermute | solution.py:16
  47.9 60.6 %collective-permute-start.9 = (bf16[2,128,4096]{2,1,0:T(8,128)(2,1)}, bf16[2,128,4096]{2,1,0:T(8,128)(2,1)}, u32[]{:S(2)}, u32[]{:S(2)}) collective-permute-start(bf16[2,128,4096]{2,1,0:T(8,128)(2,1)} %collective-permute-done.8), channel_id=1, source_target_pairs={{0,31},{1,0},{2,1},{3,2},{4,3},{5,4},{6,5},{7,6},{8,7},{9,8},{10,9... | collective-permute-start | bytes 6291464 | tf_op jit(solution)/shard_map/ppermute | solution.py:21
  65.1 88.3 %collective-permute-start.1 = (bf16[2,128,4096]{2,1,0:T(8,128)(2,1)}, bf16[2,128,4096]{2,1,0:T(8,128)(2,1)}, u32[]{:S(2)}, u32[]{:S(2)}) collective-permute-start(bf16[2,128,4096]{2,1,0:T(8,128)(2,1)} %collective-permute-done), channel_id=1, source_target_pairs={{0,31},{1,0},{2,1},{3,2},{4,3},{5,4},{6,5},{7,6},{8,7},{9,8},{10,9... | collective-permute-start | bytes 6291464 | tf_op jit(solution)/shard_map/ppermute | solution.py:21
  108.5 89.9 %collective-permute-start.10 = (bf16[2,128,4096]{2,1,0:T(8,128)(2,1)}, bf16[2,128,4096]{2,1,0:T(8,128)(2,1)S(1)}, u32[]{:S(2)}, u32[]{:S(2)}) collective-permute-start(bf16[2,128,4096]{2,1,0:T(8,128)(2,1)} %collective-permute-done.9), channel_id=1, source_target_pairs={{0,31},{1,0},{2,1},{3,2},{4,3},{5,4},{6,5},{7,6},{8,7},{9,8},{10,9... | collective-permute-start | bytes 6291464 | tf_op jit(solution)/shard_map/ppermute | solution.py:21
  153.5 89.9 %collective-permute-start.2 = (bf16[2,128,4096]{2,1,0:T(8,128)(2,1)}, bf16[2,128,4096]{2,1,0:T(8,128)(2,1)}, u32[]{:S(2)}, u32[]{:S(2)}) collective-permute-start(bf16[2,128,4096]{2,1,0:T(8,128)(2,1)} %collective-permute-done.1), channel_id=1, source_target_pairs={{0,31},{1,0},{2,1},{3,2},{4,3},{5,4},{6,5},{7,6},{8,7},{9,8},{10,9... | collective-permute-start | bytes 6291464 | tf_op jit(solution)/shard_map/ppermute | solution.py:21
  198.4 1.3 copy-start.1
  211.9 54.0 %collective-permute-start.11 = (bf16[128,4096]{1,0:T(8,128)(2,1)}, bf16[128,4096]{1,0:T(8,128)(2,1)}, u32[]{:S(2)}, u32[]{:S(2)}) collective-permute-start(bf16[128,4096]{1,0:T(8,128)(2,1)} %dynamic-slice_bitcast_fusion), channel_id=1, source_target_pairs={{0,31},{1,0},{2,1},{3,2},{4,3},{5,4},{6,5},{7,6},{8,7},{9,8},{10,9... | collective-permute-start | bytes 3145736 | tf_op jit(solution)/shard_map/ppermute | solution.py:21
  254.5 13.0 %copy-start.2 = (bf16[2,128,4096]{2,1,0:T(8,128)(2,1)S(1)}, bf16[2,128,4096]{2,1,0:T(8,128)(2,1)}, u32[]{:S(2)}) copy-start(bf16[2,128,4096]{2,1,0:T(8,128)(2,1)} %copy-done.1) | copy-start | bytes 6291460
  257.0 31.3 %collective-permute-start.3 = (bf16[128,4096]{1,0:T(8,128)(2,1)}, bf16[128,4096]{1,0:T(8,128)(2,1)S(1)}, u32[]{:S(2)}, u32[]{:S(2)}) collective-permute-start(bf16[128,4096]{1,0:T(8,128)(2,1)} %dynamic-slice_bitcast_fusion.1), channel_id=1, source_target_pairs={{0,31},{1,0},{2,1},{3,2},{4,3},{5,4},{6,5},{7,6},{8,7},{9,8},{10,9... | collective-permute-start | bytes 3145736 | tf_op jit(solution)/shard_map/ppermute | solution.py:21
  283.1 26.4 %collective-permute-start.12 = (f32[2]{0:T(128)S(1)}, f32[2]{0:T(128)S(1)}, u32[]{:S(2)}, u32[]{:S(2)}) collective-permute-start(f32[2]{0:T(128)S(1)} %fusion.107), channel_id=1, source_target_pairs={{0,1},{1,2},{2,3},{3,4},{4,5},{5,6},{6,7},{7,8},{8,9},{9,10},{10,1... | collective-permute-start | bytes 32 | tf_op jit(solution)/shard_map/ppermute | solution.py:21
  285.1 50.9 %collective-permute-start.20 = (f32[2,128]{1,0:T(2,128)S(1)}, f32[2,128]{1,0:T(2,128)S(1)}, u32[]{:S(2)}, u32[]{:S(2)}) collective-permute-start(f32[2,128]{1,0:T(2,128)S(1)} %broadcast_select_fusion.8), channel_id=1, source_target_pairs={{0,1},{1,2},{2,3},{3,4},{4,5},{5,6},{6,7},{7,8},{8,9},{9,10},{10,1... | collective-permute-start | bytes 3080 | tf_op jit(solution)/shard_map/ppermute | solution.py:21
  305.7 7.0 %collective-permute-start.4 = (f32[2]{0:T(128)S(1)}, f32[2]{0:T(128)S(1)}, u32[]{:S(2)}, u32[]{:S(2)}) collective-permute-start(f32[2]{0:T(128)S(1)} %fusion.103), channel_id=1, source_target_pairs={{0,1},{1,2},{2,3},{3,4},{4,5},{5,6},{6,7},{7,8},{8,9},{9,10},{10,1... | collective-permute-start | bytes 32 | tf_op jit(solution)/shard_map/ppermute | solution.py:21
  307.6 31.0 %collective-permute-start.16 = (f32[2,128]{1,0:T(2,128)S(1)}, f32[2,128]{1,0:T(2,128)S(1)}, u32[]{:S(2)}, u32[]{:S(2)}) collective-permute-start(f32[2,128]{1,0:T(2,128)S(1)} %broadcast_select_fusion.9), channel_id=1, source_target_pairs={{0,1},{1,2},{2,3},{3,4},{4,5},{5,6},{6,7},{7,8},{8,9},{9,10},{10,1... | collective-permute-start | bytes 3080 | tf_op jit(solution)/shard_map/ppermute | solution.py:21
  309.6 7.0 %collective-permute-start.13 = (f32[2]{0:T(128)S(1)}, f32[2]{0:T(128)S(1)}, u32[]{:S(2)}, u32[]{:S(2)}) collective-permute-start(f32[2]{0:T(128)S(1)} %add_add_fusion.2), channel_id=1, source_target_pairs={{0,1},{1,2},{2,3},{3,4},{4,5},{5,6},{6,7},{7,8},{8,9},{9,10},{10,1... | collective-permute-start | bytes 32 | tf_op jit(solution)/shard_map/ppermute | solution.py:21
  312.7 7.7 %collective-permute-start.5 = (f32[2]{0:T(128)S(1)}, f32[2]{0:T(128)S(1)}, u32[]{:S(2)}, u32[]{:S(2)}) collective-permute-start(f32[2]{0:T(128)S(1)} %add_add_fusion.5), channel_id=1, source_target_pairs={{0,1},{1,2},{2,3},{3,4},{4,5},{5,6},{6,7},{7,8},{8,9},{9,10},{10,1... | collective-permute-start | bytes 32 | tf_op jit(solution)/shard_map/ppermute | solution.py:21
  316.6 7.0 %collective-permute-start.14 = (f32[2]{0:T(128)S(1)}, f32[2]{0:T(128)S(1)}, u32[]{:S(2)}, u32[]{:S(2)}) collective-permute-start(f32[2]{0:T(128)S(1)} %add_add_fusion.1), channel_id=1, source_target_pairs={{0,1},{1,2},{2,3},{3,4},{4,5},{5,6},{6,7},{7,8},{8,9},{9,10},{10,1... | collective-permute-start | bytes 32 | tf_op jit(solution)/shard_map/ppermute | solution.py:21
  320.4 6.4 %collective-permute-start.6 = (f32[2]{0:T(128)S(1)}, f32[2]{0:T(128)S(1)}, u32[]{:S(2)}, u32[]{:S(2)}) collective-permute-start(f32[2]{0:T(128)S(1)} %add_add_fusion.4), channel_id=1, source_target_pairs={{0,1},{1,2},{2,3},{3,4},{4,5},{5,6},{6,7},{7,8},{8,9},{9,10},{10,1... | collective-permute-start | bytes 32 | tf_op jit(solution)/shard_map/ppermute | solution.py:21
  323.6 33.2 %collective-permute-start.15 = (f32[2]{0:T(128)S(1)}, f32[2]{0:T(128)S(1)}, u32[]{:S(2)}, u32[]{:S(2)}) collective-permute-start(f32[2]{0:T(128)S(1)} %add_add_fusion), channel_id=1, source_target_pairs={{0,64},{32,96},{64,0},{96,32},{128,192},{160,224},{192,128},{224,1... | collective-permute-start | bytes 32 | tf_op jit(solution)/shard_map/ppermute | solution.py:16
  326.9 30.0 %collective-permute-start.7 = (f32[2]{0:T(128)S(1)}, f32[2]{0:T(128)S(1)}, u32[]{:S(2)}, u32[]{:S(2)}) collective-permute-start(f32[2]{0:T(128)S(1)} %add_add_fusion.3), channel_id=1, source_target_pairs={{0,32},{32,0},{64,96},{96,64},{128,160},{160,128},{192,224},{224,1... | collective-permute-start | bytes 32 | tf_op jit(solution)/shard_map/ppermute | solution.py:16
  336.1 6.4 %collective-permute-start.21 = (f32[2,128]{1,0:T(2,128)S(1)}, f32[2,128]{1,0:T(2,128)S(1)}, u32[]{:S(2)}, u32[]{:S(2)}) collective-permute-start(f32[2,128]{1,0:T(2,128)S(1)} %fusion.97), channel_id=1, source_target_pairs={{0,1},{1,2},{2,3},{3,4},{4,5},{5,6},{6,7},{7,8},{8,9},{9,10},{10,1... | collective-permute-start | bytes 3080 | tf_op jit(solution)/shard_map/ppermute | solution.py:21
  338.7 6.6 %collective-permute-start.17 = (f32[2,128]{1,0:T(2,128)S(1)}, f32[2,128]{1,0:T(2,128)S(1)}, u32[]{:S(2)}, u32[]{:S(2)}) collective-permute-start(f32[2,128]{1,0:T(2,128)S(1)} %fusion.93), channel_id=1, source_target_pairs={{0,1},{1,2},{2,3},{3,4},{4,5},{5,6},{6,7},{7,8},{8,9},{9,10},{10,1... | collective-permute-start | bytes 3080 | tf_op jit(solution)/shard_map/ppermute | solution.py:21
  342.6 6.4 %collective-permute-start.22 = (f32[2,128]{1,0:T(2,128)S(1)}, f32[2,128]{1,0:T(2,128)S(1)}, u32[]{:S(2)}, u32[]{:S(2)}) collective-permute-start(f32[2,128]{1,0:T(2,128)S(1)} %fusion.98), channel_id=1, source_target_pairs={{0,1},{1,2},{2,3},{3,4},{4,5},{5,6},{6,7},{7,8},{8,9},{9,10},{10,1... | collective-permute-start | bytes 3080 | tf_op jit(solution)/shard_map/ppermute | solution.py:21
  345.3 6.9 %collective-permute-start.18 = (f32[2,128]{1,0:T(2,128)S(1)}, f32[2,128]{1,0:T(2,128)S(1)}, u32[]{:S(2)}, u32[]{:S(2)}) collective-permute-start(f32[2,128]{1,0:T(2,128)S(1)} %fusion.94), channel_id=1, source_target_pairs={{0,1},{1,2},{2,3},{3,4},{4,5},{5,6},{6,7},{7,8},{8,9},{9,10},{10,1... | collective-permute-start | bytes 3080 | tf_op jit(solution)/shard_map/ppermute | solution.py:21
  349.1 8.4 %collective-permute-start.23 = (f32[2,128]{1,0:T(2,128)S(1)}, f32[2,128]{1,0:T(2,128)S(1)}, u32[]{:S(2)}, u32[]{:S(2)}) collective-permute-start(f32[2,128]{1,0:T(2,128)S(1)} %fusion.99), channel_id=1, source_target_pairs={{0,64},{32,96},{64,0},{96,32},{128,192},{160,224},{192,128},{224,1... | collective-permute-start | bytes 3080 | tf_op jit(solution)/shard_map/ppermute | solution.py:16
  352.4 5.3 %collective-permute-start.19 = (f32[2,128]{1,0:T(2,128)S(1)}, f32[2,128]{1,0:T(2,128)S(1)}, u32[]{:S(2)}, u32[]{:S(2)}) collective-permute-start(f32[2,128]{1,0:T(2,128)S(1)} %fusion.95), channel_id=1, source_target_pairs={{0,32},{32,0},{64,96},{96,64},{128,160},{160,128},{192,224},{224,1... | collective-permute-start | bytes 3080 | tf_op jit(solution)/shard_map/ppermute | solution.py:16
where the time goes:
time: 360 us; the launch traced here: 358 us
  waiting for transfers between devices  147 us (41%)
  starting transfers between devices  106 us (29%)
  other arithmetic  48.4 us (13%)
  between operations  30.4 us (8%)
  matrix products  20 us (6%)
  local copies, waits for them, and re-layouts  6.13 us (2%)
    ppermute x18, waiting for transfers between devices, passed_along(): lax.ppermute(value, axis, [(i, (i + by) % count) for i in range(count)])  113 us
    ppermute x18, starting transfers between devices, passed_along(): lax.ppermute(value, axis, [(i, (i + by) % count) for i in range(count)])  75.6 us
    ppermute x6, waiting for transfers between devices, from_partner(): return lax.ppermute(value, axis, pairs)  34 us
    ppermute x6, starting transfers between devices, from_partner(): return lax.ppermute(value, axis, pairs)  30.7 us
    dot_general x14, matrix products, score_pair(): jnp.einsum('td,ud->tu', own_block, other_block, preferred_element_type=jn...  20 us
    reduce_sum x8, other arithmetic, score_pair(): jnp.sum(jnp.where(own_valid, row_best, 0.0)) / own_len.astype(jnp.float32)  10.1 us
    another operation x8, other arithmetic, body(): jnp.maximum(outgoing_max[offset], column_best[None, :])  9.65 us
    lt x10, other arithmetic, score_pair(): other_valid = positions < other_len  8.49 us
  transfers between devices with their start and end apart: 24, of which 12 were waited for; matrix products, arithmetic and copies ran while one was open for 19% of the time, Pallas kernels for 0%

commit v1 on v0

v1 whole, which is shorter than its diff:
```python
import functools

import jax
import jax.numpy as jnp
from jax import lax
from jax.experimental import pallas as pl
from jax.experimental.pallas import tpu as pltpu
from jax.sharding import PartitionSpec as P


epsilon = 1e-06
sentinel = -4.0


def is_mid(g):
    return (g % 2) ^ (g // 2 % 2) == 1


def side(g):
    return 1 - 2 * (g // 2 % 2)


def move(value, target):
    groups, members = lax.axis_size("grp"), lax.axis_size("dev")
    pairs = []
    for g in range(groups):
        for i in range(members):
            to = target(g, i)
            if to is not None:
                pairs.append((g * members + i, to[0] * members + to[1] % members))
    return lax.ppermute(value, ("grp", "dev"), pairs)


def along(by, mids_only):
    def target(g, i):
        return (g, i + side(g) * by) if is_mid(g) or not mids_only else None

    return target


def to_mid(mask):
    return lambda g, i: None if is_mid(g) else (g ^ mask, i)


def to_outer(mask):
    return lambda g, i: (g ^ mask, i) if is_mid(g) else None


def last_move(g, i):
    return (g, i + side(g) * (2 if is_mid(g) else 1))


def normalize_kernel(flag_ref, states_ref, both_ref, first_ref, second_ref, mixed_ref):
    units = []
    for prompt in range(2):
        values = states_ref[prompt].astype(jnp.float32)
        total = jnp.sum(values * values, axis=-1, keepdims=True)
        units.append((values * lax.rsqrt(total + epsilon)).astype(jnp.bfloat16))
        both_ref[prompt] = units[prompt]
    first_ref[...] = units[0]
    second_ref[...] = units[1]

    @pl.when(flag_ref[0] == 1)
    def _():
        mixed_ref[...] = units[0]

    @pl.when(flag_ref[0] == 0)
    def _():
        mixed_ref[...] = units[1]


def normalize(flag, states):
    _, tokens, width = states.shape
    step = 32
    block = pl.BlockSpec((2, step, width), lambda i: (0, i, 0))
    flat = pl.BlockSpec((step, width), lambda i: (i, 0))
    one = jax.ShapeDtypeStruct((tokens, width), jnp.bfloat16)
    return pl.pallas_call(
        normalize_kernel,
        grid=(tokens // step,),
        in_specs=[pl.BlockSpec(memory_space=pltpu.SMEM), block],
        out_specs=[block, flat, flat, flat],
        out_shape=[jax.ShapeDtypeStruct(states.shape, jnp.bfloat16), one, one, one],
        compiler_params=pltpu.CompilerParams(vmem_limit_bytes=32 * 1024 * 1024),
        name="normalize",
    )(flag, states)


def pair_stats(similarity, x_len, m_len):
    down = lax.broadcasted_iota(jnp.int32, similarity.shape, 0)
    lane = lax.broadcasted_iota(jnp.int32, (1, similarity.shape[1]), 1)
    m_best = jnp.max(jnp.where(down < x_len, similarity, sentinel), axis=0, keepdims=True)
    x_best = jnp.max(jnp.where(down < m_len, similarity.T, sentinel), axis=0, keepdims=True)
    x_sum = jnp.sum(jnp.where(lane < x_len, x_best, 0.0), axis=1, keepdims=True)
    m_sum = jnp.sum(jnp.where(lane < m_len, m_best, 0.0), axis=1, keepdims=True)
    x_count = jnp.full((1, 1), x_len, jnp.int32).astype(jnp.float32)
    m_count = jnp.full((1, 1), m_len, jnp.int32).astype(jnp.float32)
    score = 0.5 * (x_sum / x_count + m_sum / m_count)
    return x_best, m_best, jnp.broadcast_to(score, x_best.shape)


def score_kernel(plan, x_count, m_count, assemble, lens_ref, *refs):
    x_refs = refs[:x_count]
    m_refs = refs[x_count : x_count + m_count]
    rest = refs[x_count + m_count : -m_count]
    sums = refs[-m_count:]
    step = pl.program_id(0)
    tokens = m_refs[0].shape[-2]

    def rows(ref):
        return ref[0] if len(ref.shape) == 3 else ref[...]

    for m in range(m_count):
        stack = jnp.concatenate([rows(x_refs[x]) for x in plan[m]], axis=0)
        part = lax.dot_general(
            stack, rows(m_refs[m]), (((1,), (1,)), ((), ())), preferred_element_type=jnp.float32
        )

        @pl.when(step == 0)
        def _():
            sums[m][...] = part

        @pl.when(step > 0)
        def _():
            sums[m][...] += part

    @pl.when(step == pl.num_programs(0) - 1)
    def _():
        x_best, x_sum = [None] * x_count, [None] * x_count
        m_best, m_sum = [None] * m_count, [None] * m_count

        def join(bests, totals, at, best, score):
            bests[at] = best if bests[at] is None else jnp.maximum(bests[at], best)
            totals[at] = score if totals[at] is None else totals[at] + score

        for m in range(m_count):
            for place, x in enumerate(plan[m]):
                similarity = sums[m][place * tokens : (place + 1) * tokens, :]
                x_row, m_row, score = pair_stats(similarity, lens_ref[x], lens_ref[x_count + m])
                join(x_best, x_sum, x, x_row, score)
                join(m_best, m_sum, m, m_row, score)
        assemble(x_best, x_sum, m_best, m_sum, *rest)


def score(name, plan, lens, x_blocks, m_blocks, assemble, tables, out_rows):
    chunks = 4
    blocks = list(x_blocks) + list(m_blocks)
    arrays, specs = [], []
    for block in blocks:
        if isinstance(block, tuple):
            array, prompt = block
            _, tokens, width = array.shape
            specs.append(
                pl.BlockSpec((1, tokens, width // chunks), functools.partial(lambda p, i: (p, 0, i), prompt))
            )
        else:
            array = block
            tokens, width = array.shape
            specs.append(pl.BlockSpec((tokens, width // chunks), lambda i: (0, i)))
        arrays.append(array)
    pairs = sum(len(p) for p in plan)
    whole = [pl.BlockSpec(table.shape, lambda i: (0, 0)) for table in tables]
    return pl.pallas_call(
        functools.partial(score_kernel, plan, len(x_blocks), len(m_blocks), assemble),
        grid=(chunks,),
        in_specs=[pl.BlockSpec(memory_space=pltpu.SMEM)] + specs + whole,
        out_specs=[pl.BlockSpec((r, tokens), lambda i: (0, 0)) for r in out_rows],
        out_shape=[jax.ShapeDtypeStruct((r, tokens), jnp.float32) for r in out_rows],
        scratch_shapes=[pltpu.VMEM((len(p) * tokens, tokens), jnp.float32) for p in plan],
        cost_estimate=pl.CostEstimate(
            flops=2 * pairs * tokens * tokens * width,
            bytes_accessed=2 * len(blocks) * tokens * width,
            transcendentals=0,
        ),
        compiler_params=pltpu.CompilerParams(vmem_limit_bytes=32 * 1024 * 1024),
        name=name,
    )(lens, *arrays, *tables)


def write_near(x_best, x_sum, m_best, m_sum, out_ref):
    rows = [x_best[0], x_sum[0], x_best[1], x_sum[1]]
    for m in range(3):
        rows += [m_best[m], m_sum[m]]
    out_ref[...] = jnp.concatenate(rows + [jnp.zeros_like(rows[0])] * 6, axis=0)


def write_far_first(x_best, x_sum, m_best, m_sum, near0, near1, forth_ref, back_ref, far_ref):
    zero = jnp.zeros_like(x_best[0])
    forth = [near0[8:9], near1[8:9], near0[9:10], near1[9:10], x_best[3], x_sum[3], zero, zero]
    back = [near0[6:7], near1[6:7], near0[7:8], near1[7:8], x_best[2], x_sum[2], zero, zero]
    far = [x_best[0], x_sum[0], x_best[1], x_sum[1], m_best[0], m_sum[0], m_best[1], m_sum[1]]
    forth_ref[...] = jnp.concatenate(forth, axis=0)
    back_ref[...] = jnp.concatenate(back, axis=0)
    far_ref[...] = jnp.concatenate(far, axis=0)


def write_far_second(
    x_best, x_sum, m_best, m_sum, near0, near1, far, forth, back, core_ref, cross_ref, behind_ref, ahead_ref
):
    zero = jnp.zeros_like(x_best[0])
    for x, carried, out_ref in ((0, back, core_ref), (1, forth, cross_ref)):
        best, total = slice(2 * x, 2 * x + 1), slice(2 * x + 1, 2 * x + 2)
        out_ref[...] = jnp.concatenate(
            [
                jnp.maximum(jnp.maximum(near0[best], far[best]), carried[4:5]),
                jnp.maximum(near1[best], x_best[x]),
                near0[total] + far[total] + carried[5:6],
                near1[total] + x_sum[x],
                x_best[2 + x],
                x_sum[2 + x],
                zero,
                zero,
            ],
            axis=0,
        )
    for m, out_ref in ((0, behind_ref), (1, ahead_ref)):
        best, total = slice(4 + 2 * m, 5 + 2 * m), slice(5 + 2 * m, 6 + 2 * m)
        out_ref[...] = jnp.concatenate(
            [far[best], m_best[m], far[total], m_sum[m], zero, zero, zero, zero], axis=0
        )


def body(states, lengths):
    tokens = states.shape[2]
    candidates = lengths.shape[1]
    members = lax.axis_size("dev")
    group = lax.axis_index("grp")
    member = lax.axis_index("dev")
    high = group // 2 % 2
    mid = (group % 2) ^ high
    direction = 1 - 2 * high

    both, first, second, mixed = normalize(jnp.reshape(mid, (1,)).astype(jnp.int32), states[:, 0])

    behind1_first = move(first, along(1, False))
    ahead1_mixed = move(mixed, along(-1, False))
    cross = move(both, to_mid(2))
    behind1_second = move(second, along(1, True))
    ahead1_second = move(second, along(-1, True))
    core = move(both, to_mid(1))
    behind2_first = move(behind1_first, along(1, True))
    cross_next_first = move(behind1_first, to_mid(2))
    core_next_first = move(behind1_first, to_mid(1))
    ahead2_first = move(ahead1_mixed, along(-1, True))
    cross_next_second = move(ahead1_mixed, to_mid(2))
    core_next_second = move(ahead1_mixed, to_mid(1))
    behind2_second = move(behind1_second, along(1, True))
    ahead2_second = move(ahead1_second, along(-1, True))

    def wanted(prompt, which, place):
        return prompt * candidates + which * members + (member + direction * place) % members

    core_group, cross_group = group ^ 1, group ^ 2
    slots = []
    for prompt in range(2):
        slots += [wanted(prompt, core_group, 0), wanted(prompt, cross_group, 0)]
        slots += [wanted(prompt, group, 0), wanted(prompt, group, -1), wanted(prompt, group, 1)]
        turn = 1 if prompt == 0 else -1
        slots += [wanted(prompt, core_group, 0), wanted(prompt, cross_group, 0)]
        slots += [wanted(prompt, core_group, -turn), wanted(prompt, cross_group, turn)]
        slots += [wanted(prompt, group, -2), wanted(prompt, group, 2)]
    flat = lengths.reshape(1, -1)
    chosen = jnp.stack(slots)[:, None] == lax.broadcasted_iota(jnp.int32, (1, flat.shape[1]), 1)
    lens = jnp.sum(jnp.where(chosen, flat, 0), axis=1)

    (near0,) = score(
        "near_first", [[0, 1]] * 3, lens[0:5], [(core, 0), (cross, 0)],
        [first, behind1_first, ahead1_mixed], write_near, [], [16],
    )
    (near1,) = score(
        "near_second", [[0, 1]] * 3, lens[11:16], [(core, 1), (cross, 1)],
        [second, behind1_second, ahead1_second], write_near, [], [16],
    )
    forth, back, far = score(
        "far_first", [[0, 1, 3], [0, 1, 2]], lens[5:11],
        [(core, 0), (cross, 0), core_next_first, cross_next_first],
        [behind2_first, ahead2_first], write_far_first, [near0, near1], [8, 8, 8],
    )
    forth = move(forth, along(1, True))
    back = move(back, along(-1, True))
    to_core, to_cross, behind, ahead = score(
        "far_second", [[0, 1, 2], [0, 1, 3]], lens[16:22],
        [(core, 1), (cross, 1), core_next_second, cross_next_second],
        [behind2_second, ahead2_second], write_far_second, [near0, near1, far, forth, back], [8, 8, 8, 8],
    )
    to_core = move(to_core, to_outer(1))
    to_cross = move(to_cross, to_outer(2))
    behind = move(behind, along(-2, True))
    nothing = jnp.full((1, tokens), sentinel, jnp.float32)
    none = jnp.zeros((1, tokens), jnp.float32)
    handed = jnp.concatenate(
        [nothing, jnp.maximum(to_core[4:5], to_cross[4:5]), none, to_core[5:6] + to_cross[5:6], none, none, none, none]
    )
    is_mid_here = mid == 1
    ahead = move(jnp.where(is_mid_here, ahead, handed), last_move)

    own_best = jnp.concatenate([near0[4:5], near1[4:5]])
    own_sum = jnp.concatenate([near0[5:6], near1[5:6]])
    mid_best = jnp.maximum(jnp.maximum(own_best, forth[0:2]), jnp.maximum(back[0:2], behind[0:2]))
    mid_sum = own_sum + forth[2:4] + back[2:4] + behind[2:4]
    best = jnp.where(is_mid_here, mid_best, jnp.maximum(to_core[0:2], to_cross[0:2]))
    total = jnp.where(is_mid_here, mid_sum, to_core[2:4] + to_cross[2:4])
    best = jnp.maximum(best, ahead[0:2])
    total = total + ahead[2:4]

    own = group * members + member
    columns = lax.broadcasted_iota(jnp.int32, lengths.shape, 1)
    own_lengths = jnp.sum(jnp.where(columns == own, lengths, 0), axis=1)
    token_valid = lax.broadcasted_iota(jnp.int32, (1, tokens), 1) < own_lengths[:, None]
    best = jnp.where(token_valid, best, 0.0)
    return (total[:, :1], best[:, None, :])


def solution(mesh):
    in_specs = (P(None, ("grp", "dev"), None, None), P())
    out_specs = (P(None, ("grp", "dev")), P(None, ("grp", "dev"), None))
    return jax.shard_map(body, mesh=mesh, in_specs=in_specs, out_specs=out_specs, check_vma=False)
```

time: 360 us -> 141 us (0.39)
  the two profiles are of different devices: /device:TPU:1 before, /device:TPU:4 now
where the time goes in v1:
time: 141 us; the launch traced here: 140 us
  starting transfers between devices  59.8 us (42%)
  waiting for transfers between devices  36.5 us (26%)
  Pallas kernels  26.4 us (19%)
  local copies, waits for them, and re-layouts  15.3 us (11%)
    ppermute x20, starting transfers between devices, move(): return lax.ppermute(value, ('grp', 'dev'), pairs)  59.8 us
    ppermute x20, waiting for transfers between devices, move(): return lax.ppermute(value, ('grp', 'dev'), pairs)  36.5 us
    pallas_call x4, Pallas kernels, score(): pl.pallas_call(functools.partial(score_kernel, plan, len(x_blocks), len(m...  25.1 us
    unnamed x38, local copies, waits for them, and re-layouts  15.1 us
  transfers between devices with their start and end apart: 20, of which 5 were waited for; matrix products, arithmetic and copies ran while one was open for 0% of the time, Pallas kernels for 13%

profile of v1, /device:TPU:4, one launch (start us, length us, event | category | flops | bytes accessed | tf_op | source)
XLA Modules:
  0.0 140.1 jit_solution(14448937862614375893)
XLA Ops:
  0.7 1.6 %copy-done.4 = bf16[2,1,128,4096]{3,2,1,0:T(8,128)(2,1)S(1)} copy-done((bf16[2,1,128,4096]{3,2,1,0:T(8,128)(2,1)S(1)}, bf16[2,1,128,4096]{3,2,1,0:T(8,128)(2,1)}, u32[]{:S(2)}) %copy-start.4) | copy-done | bytes 2097176
  2.3 1.4 normalize.1
  3.7 3.8 %collective-permute-start.2 = (bf16[128,4096]{1,0:T(8,128)(2,1)S(1)}, bf16[128,4096]{1,0:T(8,128)(2,1)S(1)}, u32[]{:S(2)}, u32[]{:S(2)}) collective-permute-start(bf16[128,4096]{1,0:T(8,128)(2,1)S(1)} %get-tuple-element.14.refs_2_), channel_id=1, source_target_pairs={{0,1},{1,2},{2,3},{3,4},{4,5},{5,6},{6,7},{7,8},{8,9},{9,10},{10,1... | collective-permute-start | bytes 3145736 | tf_op jit(solution)/shard_map/ppermute | solution.py:31
  8.5 1.6 %collective-permute-start = (bf16[2,128,4096]{2,1,0:T(8,128)(2,1)S(1)}, bf16[2,128,4096]{2,1,0:T(8,128)(2,1)S(1)}, u32[]{:S(2)}, u32[]{:S(2)}) collective-permute-start(bf16[2,128,4096]{2,1,0:T(8,128)(2,1)S(1)} %get-tuple-element.13), channel_id=1, source_target_pairs={{0,32},{1,33},{2,34},{3,35},{4,36},{5,37},{6,38},{7,39},{8,40},{9,... | collective-permute-start | bytes 6291464 | tf_op jit(solution)/shard_map/ppermute | solution.py:31
  10.1 11.5 %collective-permute-start.1 = (bf16[2,128,4096]{2,1,0:T(8,128)(2,1)S(1)}, bf16[2,128,4096]{2,1,0:T(8,128)(2,1)S(1)}, u32[]{:S(2)}, u32[]{:S(2)}) collective-permute-start(bf16[2,128,4096]{2,1,0:T(8,128)(2,1)S(1)} %get-tuple-element.13), channel_id=1, source_target_pairs={{0,64},{1,65},{2,66},{3,67},{4,68},{5,69},{6,70},{7,71},{8,72},{9,... | collective-permute-start | bytes 6291464 | tf_op jit(solution)/shard_map/ppermute | solution.py:31
  21.6 2.9 %collective-permute-start.3 = (bf16[128,4096]{1,0:T(8,128)(2,1)S(1)}, bf16[128,4096]{1,0:T(8,128)(2,1)}, u32[]{:S(2)}, u32[]{:S(2)}) collective-permute-start(bf16[128,4096]{1,0:T(8,128)(2,1)S(1)} %get-tuple-element.15), channel_id=1, source_target_pairs={{0,31},{1,0},{2,1},{3,2},{4,3},{5,4},{6,5},{7,6},{8,7},{9,8},{10,9... | collective-permute-start | bytes 3145736 | tf_op jit(solution)/shard_map/ppermute | solution.py:31
  24.5 1.7 %collective-permute-start.4 = (bf16[128,4096]{1,0:T(8,128)(2,1)S(1)}, bf16[128,4096]{1,0:T(8,128)(2,1)}, u32[]{:S(2)}, u32[]{:S(2)}) collective-permute-start(bf16[128,4096]{1,0:T(8,128)(2,1)S(1)} %get-tuple-element.16.refs_2_), channel_id=1, source_target_pairs={{32,33},{33,34},{34,35},{35,36},{36,37},{37,38},{38,39},{39,40},{4... | collective-permute-start | bytes 3145736 | tf_op jit(solution)/shard_map/ppermute | solution.py:31
  26.2 13.5 %collective-permute-done.2.refs_3_ = bf16[128,4096]{1,0:T(8,128)(2,1)S(1)} collective-permute-done((bf16[128,4096]{1,0:T(8,128)(2,1)S(1)}, bf16[128,4096]{1,0:T(8,128)(2,1)S(1)}, u32[]{:S(2)}, u32[]{:S(2)}) %collective-permute-start.2) | collective-permute-done | bytes 1048608 | tf_op jit(solution)/shard_map/ppermute | solution.py:31
  39.7 1.7 %collective-permute-start.5 = (bf16[128,4096]{1,0:T(8,128)(2,1)S(1)}, bf16[128,4096]{1,0:T(8,128)(2,1)}, u32[]{:S(2)}, u32[]{:S(2)}) collective-permute-start(bf16[128,4096]{1,0:T(8,128)(2,1)S(1)} %get-tuple-element.16.refs_2_), channel_id=1, source_target_pairs={{32,63},{33,32},{34,33},{35,34},{36,35},{37,36},{38,37},{39,38},{4... | collective-permute-start | bytes 3145736 | tf_op jit(solution)/shard_map/ppermute | solution.py:31
  42.3 3.2 %collective-permute-done.3.refs_4_ = bf16[128,4096]{1,0:T(8,128)(2,1)} collective-permute-done((bf16[128,4096]{1,0:T(8,128)(2,1)S(1)}, bf16[128,4096]{1,0:T(8,128)(2,1)}, u32[]{:S(2)}, u32[]{:S(2)}) %collective-permute-start.3) | collective-permute-done | bytes 1048608 | tf_op jit(solution)/shard_map/ppermute | solution.py:31
  45.5 1.3 collective-permute-start.6
  46.8 7.1 %collective-permute-start.7 = (bf16[128,4096]{1,0:T(8,128)(2,1)S(1)}, bf16[128,4096]{1,0:T(8,128)(2,1)S(1)}, u32[]{:S(2)}, u32[]{:S(2)}) collective-permute-start(bf16[128,4096]{1,0:T(8,128)(2,1)S(1)} %collective-permute-done.2.refs_3_), channel_id=1, source_target_pairs={{0,64},{1,65},{2,66},{3,67},{4,68},{5,69},{6,70},{7,71},{8,72},{9,... | collective-permute-start | bytes 3145736 | tf_op jit(solution)/shard_map/ppermute | solution.py:31
  55.7 1.6 %collective-permute-start.9 = (bf16[128,4096]{1,0:T(8,128)(2,1)}, bf16[128,4096]{1,0:T(8,128)(2,1)}, u32[]{:S(2)}, u32[]{:S(2)}) collective-permute-start(bf16[128,4096]{1,0:T(8,128)(2,1)} %collective-permute-done.3.refs_4_), channel_id=1, source_target_pairs={{32,63},{33,32},{34,33},{35,34},{36,35},{37,36},{38,37},{39,38},{4... | collective-permute-start | bytes 3145736 | tf_op jit(solution)/shard_map/ppermute | solution.py:31
  57.3 1.4 copy-done
  58.7 8.5 %collective-permute-start.12 = (bf16[128,4096]{1,0:T(8,128)(2,1)}, bf16[128,4096]{1,0:T(8,128)(2,1)S(1)}, u32[]{:S(2)}, u32[]{:S(2)}) collective-permute-start(bf16[128,4096]{1,0:T(8,128)(2,1)} %collective-permute-done.3.refs_4_), channel_id=1, source_target_pairs={{0,32},{1,33},{2,34},{3,35},{4,36},{5,37},{6,38},{7,39},{8,40},{9,... | collective-permute-start | bytes 3145736 | tf_op jit(solution)/shard_map/ppermute | solution.py:31
  68.2 7.4 %collective-permute-start.13 = (bf16[128,4096]{1,0:T(8,128)(2,1)}, bf16[128,4096]{1,0:T(8,128)(2,1)}, u32[]{:S(2)}, u32[]{:S(2)}) collective-permute-start(bf16[128,4096]{1,0:T(8,128)(2,1)} %collective-permute-done.3.refs_4_), channel_id=1, source_target_pairs={{0,64},{1,65},{2,66},{3,67},{4,68},{5,69},{6,70},{7,71},{8,72},{9,... | collective-permute-start | bytes 3145736 | tf_op jit(solution)/shard_map/ppermute | solution.py:31
  76.6 1.6 %collective-permute-start.14 = (bf16[128,4096]{1,0:T(8,128)(2,1)}, bf16[128,4096]{1,0:T(8,128)(2,1)}, u32[]{:S(2)}, u32[]{:S(2)}) collective-permute-start(bf16[128,4096]{1,0:T(8,128)(2,1)} %collective-permute-done.4.refs_3_), channel_id=1, source_target_pairs={{32,33},{33,34},{34,35},{35,36},{36,37},{37,38},{38,39},{39,40},{4... | collective-permute-start | bytes 3145736 | tf_op jit(solution)/shard_map/ppermute | solution.py:31
  79.2 1.7 %collective-permute-start.15 = (bf16[128,4096]{1,0:T(8,128)(2,1)}, bf16[128,4096]{1,0:T(8,128)(2,1)}, u32[]{:S(2)}, u32[]{:S(2)}) collective-permute-start(bf16[128,4096]{1,0:T(8,128)(2,1)} %collective-permute-done.5.refs_4_), channel_id=1, source_target_pairs={{32,63},{33,32},{34,33},{35,34},{36,35},{37,36},{38,37},{39,38},{4... | collective-permute-start | bytes 3145736 | tf_op jit(solution)/shard_map/ppermute | solution.py:31
  81.4 1.6 %copy-done.1 = bf16[2,128,4096]{2,1,0:T(8,128)(2,1)S(1)} copy-done((bf16[2,128,4096]{2,1,0:T(8,128)(2,1)S(1)}, bf16[2,128,4096]{2,1,0:T(8,128)(2,1)}, u32[]{:S(2)}) %copy-start.1) | copy-done | bytes 2097176
  83.0 1.2 copy-done.14
  84.2 1.2 copy-done.16
  85.5 6.3 %near_first.1.refs_6_ = f32[16,128]{1,0:T(8,128)S(1)} custom-call(s32[5]{0:T(128)S(1)} %get-tuple-element.38.lens_ref, bf16[2,128,4096]{2,1,0:T(8,128)(2,1)S(1)} %collective-permute-done.refs_0_, bf16[2,128,4096]{2,1,0:T(8,128)(2,1)S(1)} %copy-done.1, bf16[128,4096]{1,0:T(8,128)(2,1)S(1)} %copy-done.14, bf16[128,4096]{1,0:T(8,128)(2,1)S(1)} %copy-done.16, ...), custom_call_target="tpu_custom_call" | custom-call | flops 805306368 | bytes 5242880 | tf_op jit(solution)/shard_map/near_first/pallas_call | solution.py:163
  91.9 6.4 %near_second.1.refs_7_ = f32[16,128]{1,0:T(8,128)S(1)} custom-call(s32[5]{0:T(128)S(1)} %get-tuple-element.39.lens_ref, bf16[2,128,4096]{2,1,0:T(8,128)(2,1)S(1)} %collective-permute-done.refs_0_, bf16[2,128,4096]{2,1,0:T(8,128)(2,1)S(1)} %copy-done.2, bf16[128,4096]{1,0:T(8,128)(2,1)S(1)} %copy-done.12, bf16[128,4096]{1,0:T(8,128)(2,1)} %collective-permute-done.4.refs_3_, ...), custom_call_target="tpu_custom_call" | custom-call | flops 805306368 | bytes 5242880 | tf_op jit(solution)/shard_map/near_second/pallas_call | solution.py:163
  98.3 6.1 %far_first.1 = (f32[8,128]{1,0:T(8,128)S(1)}, f32[8,128]{1,0:T(8,128)S(1)}, f32[8,128]{1,0:T(8,128)S(1)}) custom-call(s32[6]{0:T(128)S(1)} %get-tuple-element.36.lens_ref, bf16[2,128,4096]{2,1,0:T(8,128)(2,1)S(1)} %collective-permute-done.refs_0_, bf16[2,128,4096]{2,1,0:T(8,128)(2,1)S(1)} %copy-done.2, bf16[128,4096]{1,0:T(8,128)(2,1)S(1)} %copy-done.6, ...), custom_call_target="tpu_custom_call" | custom-call | flops 805306368 | bytes 6291456 | tf_op jit(solution)/shard_map/far_first/pallas_call | solution.py:163
  106.0 1.6 %copy-done.3 = bf16[2,128,4096]{2,1,0:T(8,128)(2,1)S(1)} copy-done((bf16[2,128,4096]{2,1,0:T(8,128)(2,1)S(1)}, bf16[2,128,4096]{2,1,0:T(8,128)(2,1)}, u32[]{:S(2)}) %copy-start.3) | copy-done | bytes 2097176
  107.5 6.2 %far_second.1 = (f32[8,128]{1,0:T(8,128)S(1)}, f32[8,128]{1,0:T(8,128)S(1)}, f32[8,128]{1,0:T(8,128)S(1)}, f32[8,128]{1,0:T(8,128)S(1)}) custom-call(s32[6]{0:T(128)S(1)} %get-tuple-element.37.lens_ref, bf16[2,128,4096]{2,1,0:T(8,128)(2,1)S(1)} %collective-permute-done.refs_0_, bf16[2,128,4096]{2,1,0:T(8,128)(2,1)S(1)} %copy-done.3, ...), custom_call_target="tpu_custom_call" | custom-call | flops 805306368 | bytes 6291456 | tf_op jit(solution)/shard_map/far_second/pallas_call | solution.py:163
  113.8 1.3 collective-permute-start.17
  115.1 1.3 collective-permute-start.18
  117.0 2.7 %collective-permute-done.17 = f32[8,128]{1,0:T(8,128)S(1)} collective-permute-done((f32[8,128]{1,0:T(8,128)S(1)}, f32[8,128]{1,0:T(8,128)S(1)}, u32[]{:S(2)}, u32[]{:S(2)}) %collective-permute-start.17) | collective-permute-done | bytes 4128 | tf_op jit(solution)/shard_map/ppermute | solution.py:31
  119.7 11.5 %collective-permute-done.18 = f32[8,128]{1,0:T(8,128)S(1)} collective-permute-done((f32[8,128]{1,0:T(8,128)S(1)}, f32[8,128]{1,0:T(8,128)S(1)}, u32[]{:S(2)}, u32[]{:S(2)}) %collective-permute-start.18) | collective-permute-done | bytes 4128 | tf_op jit(solution)/shard_map/ppermute | solution.py:31
  131.2 1.9 %collective-permute-start.19 = (f32[8,128]{1,0:T(8,128)S(1)}, f32[8,128]{1,0:T(8,128)S(1)}, u32[]{:S(2)}, u32[]{:S(2)}) collective-permute-start(f32[8,128]{1,0:T(8,128)S(1)} %broadcast_select_fusion), channel_id=1, source_target_pairs={{0,1},{1,2},{2,3},{3,4},{4,5},{5,6},{6,7},{7,8},{8,9},{9,10},{10,1... | collective-permute-start | bytes 12296 | tf_op jit(solution)/shard_map/ppermute | solution.py:31
  133.2 5.7 %collective-permute-done.19 = f32[8,128]{1,0:T(8,128)S(1)} collective-permute-done((f32[8,128]{1,0:T(8,128)S(1)}, f32[8,128]{1,0:T(8,128)S(1)}, u32[]{:S(2)}, u32[]{:S(2)}) %collective-permute-start.19) | collective-permute-done | bytes 4128 | tf_op jit(solution)/shard_map/ppermute | solution.py:31
  (66 shorter events, 10.5 us)
Async XLA Ops:
  0.6 80.3 %copy-start.17 = (s32[2,512]{1,0:T(2,128)S(1)}, s32[2,512]{1,0:T(2,128)}, u32[]{:S(2)}) copy-start(s32[2,512]{1,0:T(2,128)} %param.3) | copy-start | bytes 12292
  0.7 1.6 %copy-start.4 = (bf16[2,1,128,4096]{3,2,1,0:T(8,128)(2,1)S(1)}, bf16[2,1,128,4096]{3,2,1,0:T(8,128)(2,1)}, u32[]{:S(2)}) copy-start(bf16[2,1,128,4096]{3,2,1,0:T(8,128)(2,1)} %param.2) | copy-start | bytes 6291460
  3.7 36.0 %collective-permute-start.2 = (bf16[128,4096]{1,0:T(8,128)(2,1)S(1)}, bf16[128,4096]{1,0:T(8,128)(2,1)S(1)}, u32[]{:S(2)}, u32[]{:S(2)}) collective-permute-start(bf16[128,4096]{1,0:T(8,128)(2,1)S(1)} %get-tuple-element.14.refs_2_), channel_id=1, source_target_pairs={{0,1},{1,2},{2,3},{3,4},{4,5},{5,6},{6,7},{7,8},{8,9},{9,10},{10,1... | collective-permute-start | bytes 3145736 | tf_op jit(solution)/shard_map/ppermute | solution.py:31
  8.5 47.2 %collective-permute-start = (bf16[2,128,4096]{2,1,0:T(8,128)(2,1)S(1)}, bf16[2,128,4096]{2,1,0:T(8,128)(2,1)S(1)}, u32[]{:S(2)}, u32[]{:S(2)}) collective-permute-start(bf16[2,128,4096]{2,1,0:T(8,128)(2,1)S(1)} %get-tuple-element.13), channel_id=1, source_target_pairs={{0,32},{1,33},{2,34},{3,35},{4,36},{5,37},{6,38},{7,39},{8,40},{9,... | collective-permute-start | bytes 6291464 | tf_op jit(solution)/shard_map/ppermute | solution.py:31
  10.1 47.3 %collective-permute-start.1 = (bf16[2,128,4096]{2,1,0:T(8,128)(2,1)S(1)}, bf16[2,128,4096]{2,1,0:T(8,128)(2,1)S(1)}, u32[]{:S(2)}, u32[]{:S(2)}) collective-permute-start(bf16[2,128,4096]{2,1,0:T(8,128)(2,1)S(1)} %get-tuple-element.13), channel_id=1, source_target_pairs={{0,64},{1,65},{2,66},{3,67},{4,68},{5,69},{6,70},{7,71},{8,72},{9,... | collective-permute-start | bytes 6291464 | tf_op jit(solution)/shard_map/ppermute | solution.py:31
  21.6 23.9 %collective-permute-start.3 = (bf16[128,4096]{1,0:T(8,128)(2,1)S(1)}, bf16[128,4096]{1,0:T(8,128)(2,1)}, u32[]{:S(2)}, u32[]{:S(2)}) collective-permute-start(bf16[128,4096]{1,0:T(8,128)(2,1)S(1)} %get-tuple-element.15), channel_id=1, source_target_pairs={{0,31},{1,0},{2,1},{3,2},{4,3},{5,4},{6,5},{7,6},{8,7},{9,8},{10,9... | collective-permute-start | bytes 3145736 | tf_op jit(solution)/shard_map/ppermute | solution.py:31
  24.5 22.3 %collective-permute-start.4 = (bf16[128,4096]{1,0:T(8,128)(2,1)S(1)}, bf16[128,4096]{1,0:T(8,128)(2,1)}, u32[]{:S(2)}, u32[]{:S(2)}) collective-permute-start(bf16[128,4096]{1,0:T(8,128)(2,1)S(1)} %get-tuple-element.16.refs_2_), channel_id=1, source_target_pairs={{32,33},{33,34},{34,35},{35,36},{36,37},{37,38},{38,39},{39,40},{4... | collective-permute-start | bytes 3145736 | tf_op jit(solution)/shard_map/ppermute | solution.py:31
  39.7 14.3 %collective-permute-start.5 = (bf16[128,4096]{1,0:T(8,128)(2,1)S(1)}, bf16[128,4096]{1,0:T(8,128)(2,1)}, u32[]{:S(2)}, u32[]{:S(2)}) collective-permute-start(bf16[128,4096]{1,0:T(8,128)(2,1)S(1)} %get-tuple-element.16.refs_2_), channel_id=1, source_target_pairs={{32,63},{33,32},{34,33},{35,34},{36,35},{37,36},{38,37},{39,38},{4... | collective-permute-start | bytes 3145736 | tf_op jit(solution)/shard_map/ppermute | solution.py:31
  45.5 21.8 %collective-permute-start.6 = (bf16[128,4096]{1,0:T(8,128)(2,1)S(1)}, bf16[128,4096]{1,0:T(8,128)(2,1)S(1)}, u32[]{:S(2)}, u32[]{:S(2)}) collective-permute-start(bf16[128,4096]{1,0:T(8,128)(2,1)S(1)} %collective-permute-done.2.refs_3_), channel_id=1, source_target_pairs={{0,32},{1,33},{2,34},{3,35},{4,36},{5,37},{6,38},{7,39},{8,40},{9,... | collective-permute-start | bytes 3145736 | tf_op jit(solution)/shard_map/ppermute | solution.py:31
  46.8 28.8 %collective-permute-start.7 = (bf16[128,4096]{1,0:T(8,128)(2,1)S(1)}, bf16[128,4096]{1,0:T(8,128)(2,1)S(1)}, u32[]{:S(2)}, u32[]{:S(2)}) collective-permute-start(bf16[128,4096]{1,0:T(8,128)(2,1)S(1)} %collective-permute-done.2.refs_3_), channel_id=1, source_target_pairs={{0,64},{1,65},{2,66},{3,67},{4,68},{5,69},{6,70},{7,71},{8,72},{9,... | collective-permute-start | bytes 3145736 | tf_op jit(solution)/shard_map/ppermute | solution.py:31
  53.9 24.3 %collective-permute-start.8 = (bf16[128,4096]{1,0:T(8,128)(2,1)S(1)}, bf16[128,4096]{1,0:T(8,128)(2,1)S(1)}, u32[]{:S(2)}, u32[]{:S(2)}) collective-permute-start(bf16[128,4096]{1,0:T(8,128)(2,1)S(1)} %collective-permute-done.2.refs_3_), channel_id=1, source_target_pairs={{32,33},{33,34},{34,35},{35,36},{36,37},{37,38},{38,39},{39,40},{4... | collective-permute-start | bytes 3145736 | tf_op jit(solution)/shard_map/ppermute | solution.py:31
  55.7 42.6 %collective-permute-start.9 = (bf16[128,4096]{1,0:T(8,128)(2,1)}, bf16[128,4096]{1,0:T(8,128)(2,1)}, u32[]{:S(2)}, u32[]{:S(2)}) collective-permute-start(bf16[128,4096]{1,0:T(8,128)(2,1)} %collective-permute-done.3.refs_4_), channel_id=1, source_target_pairs={{32,63},{33,32},{34,33},{35,34},{36,35},{37,36},{38,37},{39,38},{4... | collective-permute-start | bytes 3145736 | tf_op jit(solution)/shard_map/ppermute | solution.py:31
  57.3 1.4 copy-start
  58.7 46.4 %collective-permute-start.12 = (bf16[128,4096]{1,0:T(8,128)(2,1)}, bf16[128,4096]{1,0:T(8,128)(2,1)S(1)}, u32[]{:S(2)}, u32[]{:S(2)}) collective-permute-start(bf16[128,4096]{1,0:T(8,128)(2,1)} %collective-permute-done.3.refs_4_), channel_id=1, source_target_pairs={{0,32},{1,33},{2,34},{3,35},{4,36},{5,37},{6,38},{7,39},{8,40},{9,... | collective-permute-start | bytes 3145736 | tf_op jit(solution)/shard_map/ppermute | solution.py:31
  68.2 37.7 %collective-permute-start.13 = (bf16[128,4096]{1,0:T(8,128)(2,1)}, bf16[128,4096]{1,0:T(8,128)(2,1)}, u32[]{:S(2)}, u32[]{:S(2)}) collective-permute-start(bf16[128,4096]{1,0:T(8,128)(2,1)} %collective-permute-done.3.refs_4_), channel_id=1, source_target_pairs={{0,64},{1,65},{2,66},{3,67},{4,68},{5,69},{6,70},{7,71},{8,72},{9,... | collective-permute-start | bytes 3145736 | tf_op jit(solution)/shard_map/ppermute | solution.py:31
  76.6 29.3 %collective-permute-start.14 = (bf16[128,4096]{1,0:T(8,128)(2,1)}, bf16[128,4096]{1,0:T(8,128)(2,1)}, u32[]{:S(2)}, u32[]{:S(2)}) collective-permute-start(bf16[128,4096]{1,0:T(8,128)(2,1)} %collective-permute-done.4.refs_3_), channel_id=1, source_target_pairs={{32,33},{33,34},{34,35},{35,36},{36,37},{37,38},{38,39},{39,40},{4... | collective-permute-start | bytes 3145736 | tf_op jit(solution)/shard_map/ppermute | solution.py:31
  79.2 26.7 %collective-permute-start.15 = (bf16[128,4096]{1,0:T(8,128)(2,1)}, bf16[128,4096]{1,0:T(8,128)(2,1)}, u32[]{:S(2)}, u32[]{:S(2)}) collective-permute-start(bf16[128,4096]{1,0:T(8,128)(2,1)} %collective-permute-done.5.refs_4_), channel_id=1, source_target_pairs={{32,63},{33,32},{34,33},{35,34},{36,35},{37,36},{38,37},{39,38},{4... | collective-permute-start | bytes 3145736 | tf_op jit(solution)/shard_map/ppermute | solution.py:31
  81.4 1.6 %copy-start.1 = (bf16[2,128,4096]{2,1,0:T(8,128)(2,1)S(1)}, bf16[2,128,4096]{2,1,0:T(8,128)(2,1)}, u32[]{:S(2)}) copy-start(bf16[2,128,4096]{2,1,0:T(8,128)(2,1)} %copy-done) | copy-start | bytes 6291460
  83.0 1.2 copy-start.14
  84.2 1.2 copy-start.16
  85.5 6.3 %copy-start.2 = (bf16[2,128,4096]{2,1,0:T(8,128)(2,1)S(1)}, bf16[2,128,4096]{2,1,0:T(8,128)(2,1)}, u32[]{:S(2)}) copy-start(bf16[2,128,4096]{2,1,0:T(8,128)(2,1)} %copy-done) | copy-start | bytes 6291460
  85.5 6.4 %copy-start.12 = (bf16[128,4096]{1,0:T(8,128)(2,1)S(1)}, bf16[128,4096]{1,0:T(8,128)(2,1)}, u32[]{:S(2)}) copy-start(bf16[128,4096]{1,0:T(8,128)(2,1)} %copy-done.11) | copy-start | bytes 3145732
  91.8 6.4 %copy-start.6 = (bf16[128,4096]{1,0:T(8,128)(2,1)S(1)}, bf16[128,4096]{1,0:T(8,128)(2,1)}, u32[]{:S(2)}) copy-start(bf16[128,4096]{1,0:T(8,128)(2,1)} %copy-done.5) | copy-start | bytes 3145732
  91.8 6.4 %copy-start.8 = (bf16[128,4096]{1,0:T(8,128)(2,1)S(1)}, bf16[128,4096]{1,0:T(8,128)(2,1)}, u32[]{:S(2)}) copy-start(bf16[128,4096]{1,0:T(8,128)(2,1)} %copy-done.7) | copy-start | bytes 3145732
  91.9 6.4 %copy-start.10 = (bf16[128,4096]{1,0:T(8,128)(2,1)S(1)}, bf16[128,4096]{1,0:T(8,128)(2,1)}, u32[]{:S(2)}) copy-start(bf16[128,4096]{1,0:T(8,128)(2,1)} %copy-done.9) | copy-start | bytes 3145732
  104.4 1.5 %collective-permute-start.10 = (f32[8,128]{1,0:T(8,128)S(1)}, f32[8,128]{1,0:T(8,128)S(1)}, u32[]{:S(2)}, u32[]{:S(2)}) collective-permute-start(f32[8,128]{1,0:T(8,128)S(1)} %get-tuple-element.17), channel_id=1, source_target_pairs={{32,33},{33,34},{34,35},{35,36},{36,37},{37,38},{38,39},{39,40},{4... | collective-permute-start | bytes 12296 | tf_op jit(solution)/shard_map/ppermute | solution.py:31
  105.1 0.8 collective-permute-start.11
  106.0 1.6 %copy-start.3 = (bf16[2,128,4096]{2,1,0:T(8,128)(2,1)S(1)}, bf16[2,128,4096]{2,1,0:T(8,128)(2,1)}, u32[]{:S(2)}) copy-start(bf16[2,128,4096]{2,1,0:T(8,128)(2,1)} %copy-done) | copy-start | bytes 6291460
  113.8 5.9 %collective-permute-start.17 = (f32[8,128]{1,0:T(8,128)S(1)}, f32[8,128]{1,0:T(8,128)S(1)}, u32[]{:S(2)}, u32[]{:S(2)}) collective-permute-start(f32[8,128]{1,0:T(8,128)S(1)} %get-tuple-element.21), channel_id=1, source_target_pairs={{32,0},{33,1},{34,2},{35,3},{36,4},{37,5},{38,6},{39,7},{40,8},{41... | collective-permute-start | bytes 12296 | tf_op jit(solution)/shard_map/ppermute | solution.py:31
  115.1 16.1 %collective-permute-start.18 = (f32[8,128]{1,0:T(8,128)S(1)}, f32[8,128]{1,0:T(8,128)S(1)}, u32[]{:S(2)}, u32[]{:S(2)}) collective-permute-start(f32[8,128]{1,0:T(8,128)S(1)} %get-tuple-element.22), channel_id=1, source_target_pairs={{32,96},{33,97},{34,98},{35,99},{36,100},{37,101},{38,102},{39,103... | collective-permute-start | bytes 12296 | tf_op jit(solution)/shard_map/ppermute | solution.py:31
  116.4 16.8 %collective-permute-start.16 = (f32[8,128]{1,0:T(8,128)S(1)}, f32[8,128]{1,0:T(8,128)S(1)}, u32[]{:S(2)}, u32[]{:S(2)}) collective-permute-start(f32[8,128]{1,0:T(8,128)S(1)} %get-tuple-element.20), channel_id=1, source_target_pairs={{32,62},{33,63},{34,32},{35,33},{36,34},{37,35},{38,36},{39,37},{4... | collective-permute-start | bytes 12296 | tf_op jit(solution)/shard_map/ppermute | solution.py:31
  131.2 7.6 %collective-permute-start.19 = (f32[8,128]{1,0:T(8,128)S(1)}, f32[8,128]{1,0:T(8,128)S(1)}, u32[]{:S(2)}, u32[]{:S(2)}) collective-permute-start(f32[8,128]{1,0:T(8,128)S(1)} %broadcast_select_fusion), channel_id=1, source_target_pairs={{0,1},{1,2},{2,3},{3,4},{4,5},{5,6},{6,7},{7,8},{8,9},{9,10},{10,1... | collective-permute-start | bytes 12296 | tf_op jit(solution)/shard_map/ppermute | solution.py:31
  (6 other events, 5.9 us)

commit v2 on v0

v2 whole, which is shorter than its diff:
```python
import functools

import jax
import jax.numpy as jnp
from jax import lax
from jax.experimental import pallas as pl
from jax.experimental.pallas import tpu as pltpu
from jax.sharding import PartitionSpec as P


epsilon = 1e-06
sentinel = -4.0
VMEM_LIMIT = 24 * 1024 * 1024


def is_mid(g):
    return (g % 2) ^ (g // 2 % 2) == 1


def sign(g):
    return 2 * (g % 2) - 1


def send_home(value, way):
    groups, members = lax.axis_size("grp"), lax.axis_size("dev")
    pairs = []
    for g in range(groups):
        by = way * (1 - 2 * (g // 2 % 2)) * (2 if is_mid(g) else 1)
        for i in range(members):
            pairs.append((g * members + i, g * members + (i + by) % members))
    return lax.ppermute(value, ("grp", "dev"), pairs)


def move(value, by, mask=0):
    groups, members = lax.axis_size("grp"), lax.axis_size("dev")
    pairs = []
    for g in range(groups):
        for i in range(members):
            pairs.append((g * members + i, (g ^ mask) * members + (i + sign(g) * by) % members))
    return lax.ppermute(value, ("grp", "dev"), pairs)


def gather(value, size):
    groups = lax.axis_size("grp")
    return lax.all_gather(
        value, "grp", axis_index_groups=[list(range(g, g + size)) for g in range(0, groups, size)]
    )


def after(value, *done):
    return lax.optimization_barrier((value, *done))


def pick_kernel(flags_ref, states_ref, out_ref, sem):
    copy = pltpu.make_async_copy(states_ref.at[flags_ref[0]], out_ref, sem)
    copy.start()
    copy.wait()


def pick(flags, states):
    anywhere = pl.BlockSpec(memory_space=pl.ANY)
    return pl.pallas_call(
        pick_kernel,
        in_specs=[pl.BlockSpec(memory_space=pltpu.SMEM), anywhere],
        out_specs=pl.BlockSpec(memory_space=pltpu.VMEM),
        out_shape=jax.ShapeDtypeStruct(states.shape[1:], states.dtype),
        scratch_shapes=[pltpu.SemaphoreType.DMA],
        name="pick",
    )(flags, states)


def normalize_kernel(flags_ref, states_ref, given_ref, m_ref, c_ref, loaded, unit, load_sems, sems):
    steps = load_sems.shape[0]
    size = loaded.shape[1] // steps
    mid = flags_ref[0]

    def loads(step):
        rows = pl.ds(step * size, size)
        return (
            pltpu.make_async_copy(states_ref.at[1 - mid, rows], loaded.at[0, rows], load_sems.at[step, 0]),
            pltpu.make_async_copy(given_ref.at[rows], loaded.at[1, rows], load_sems.at[step, 1]),
        )

    def stores(step):
        rows = pl.ds(step * size, size)
        return (
            pltpu.make_async_copy(unit.at[1 - mid, rows], m_ref.at[rows], sems.at[step, 0]),
            pltpu.make_async_copy(unit.at[mid, rows], c_ref.at[rows], sems.at[step, 1]),
        )

    for step in range(steps):
        for copy in loads(step):
            copy.start()
    for step in range(steps):
        for copy in loads(step):
            copy.wait()
        rows = pl.ds(step * size, size)
        for at in range(2):
            values = loaded[at, rows].astype(jnp.float32)
            total = jnp.sum(values * values, axis=-1, keepdims=True)
            unit[at, rows] = (values * lax.rsqrt(total + epsilon)).astype(jnp.bfloat16)
        for copy in stores(step):
            copy.start()
    for step in range(steps):
        for copy in stores(step):
            copy.wait()


def normalize(flags, states, given):
    _, tokens, width = states.shape
    steps = 4
    one = jax.ShapeDtypeStruct((tokens, width), jnp.bfloat16)
    anywhere = pl.BlockSpec(memory_space=pl.ANY)
    return pl.pallas_call(
        normalize_kernel,
        in_specs=[pl.BlockSpec(memory_space=pltpu.SMEM), anywhere, anywhere],
        out_specs=[anywhere] * 2,
        out_shape=[one, one],
        scratch_shapes=[
            pltpu.VMEM(states.shape, jnp.bfloat16),
            pltpu.VMEM(states.shape, jnp.bfloat16),
            pltpu.SemaphoreType.DMA((steps, 2)),
            pltpu.SemaphoreType.DMA((steps, 2)),
        ],
        compiler_params=pltpu.CompilerParams(vmem_limit_bytes=VMEM_LIMIT),
        name="normalize",
    )(flags, states, given)


def pair_stats(similarity, x_len, m_len):
    down = lax.broadcasted_iota(jnp.int32, similarity.shape, 0)
    lane = lax.broadcasted_iota(jnp.int32, (1, similarity.shape[1]), 1)
    x_best = jnp.max(jnp.where(down < m_len, similarity, sentinel), axis=0, keepdims=True)
    m_best = jnp.max(jnp.where(down < x_len, similarity.T, sentinel), axis=0, keepdims=True)
    x_sum = jnp.sum(jnp.where(lane < x_len, x_best, 0.0), axis=1, keepdims=True)
    m_sum = jnp.sum(jnp.where(lane < m_len, m_best, 0.0), axis=1, keepdims=True)
    x_count = jnp.full((1, 1), x_len, jnp.int32).astype(jnp.float32)
    m_count = jnp.full((1, 1), m_len, jnp.int32).astype(jnp.float32)
    score = 0.5 * (x_sum / x_count + m_sum / m_count)
    return x_best, m_best, jnp.broadcast_to(score, x_best.shape)


def score_kernel(plan, at, x_count, m_count, out_count, assemble, slots_ref, *refs):
    sources = refs[: x_count + m_count]
    tables = refs[x_count + m_count : -3 - out_count]
    outs = refs[-3 - out_count : -3]
    x_stack, m_stack, sems = refs[-3:]
    tokens, width = sources[0].shape
    halves = sems.shape[1]
    size = width // halves

    def load(block, half):
        stack, row = (x_stack, block) if block < x_count else (m_stack, block - x_count)
        columns = pl.ds(half * size, size)
        return pltpu.make_async_copy(
            sources[block].at[:, columns], stack.at[pl.ds(row * tokens, tokens), columns], sems.at[block, half]
        )

    for half in range(halves):
        for block in range(x_count + m_count):
            load(block, half).start()
    similarity = None
    for half in range(halves):
        for block in range(x_count + m_count):
            load(block, half).wait()
        columns = pl.ds(half * size, size)
        part = lax.dot_general(
            m_stack[:, columns], x_stack[:, columns], (((1,), (1,)), ((), ())),
            preferred_element_type=jnp.float32,
        )
        similarity = part if similarity is None else similarity + part
    x_best, x_sum = [None] * x_count, [None] * x_count
    m_best, m_sum = [None] * m_count, [None] * m_count

    def join(bests, totals, where, best, score):
        bests[where] = best if bests[where] is None else jnp.maximum(bests[where], best)
        totals[where] = score if totals[where] is None else totals[where] + score

    for m in range(m_count):
        for x in plan[m]:
            block = similarity[m * tokens : (m + 1) * tokens, x * tokens : (x + 1) * tokens]
            x_row, m_row, score = pair_stats(block, slots_ref[at + x], slots_ref[at + x_count + m])
            join(x_best, x_sum, x, x_row, score)
            join(m_best, m_sum, m, m_row, score)
    assemble(x_best, x_sum, m_best, m_sum, *tables, *outs)


def score(name, plan, slots, at, x_blocks, m_blocks, assemble, tables, out_rows):
    arrays = list(x_blocks) + list(m_blocks)
    tokens, width = arrays[0].shape
    vmem = pl.BlockSpec(memory_space=pltpu.VMEM)
    halves = 2
    return pl.pallas_call(
        functools.partial(score_kernel, plan, at, len(x_blocks), len(m_blocks), len(out_rows), assemble),
        in_specs=[pl.BlockSpec(memory_space=pltpu.SMEM)]
        + [pl.BlockSpec(memory_space=pl.ANY)] * len(arrays)
        + [vmem] * len(tables),
        out_specs=[vmem for rows in out_rows],
        out_shape=[jax.ShapeDtypeStruct((rows, tokens), jnp.float32) for rows in out_rows],
        scratch_shapes=[
            pltpu.VMEM((len(x_blocks) * tokens, width), jnp.bfloat16),
            pltpu.VMEM((len(m_blocks) * tokens, width), jnp.bfloat16),
            pltpu.SemaphoreType.DMA((len(arrays), halves)),
        ],
        cost_estimate=pl.CostEstimate(
            flops=2 * len(x_blocks) * len(m_blocks) * tokens * tokens * width,
            bytes_accessed=2 * len(arrays) * tokens * width,
            transcendentals=0,
        ),
        compiler_params=pltpu.CompilerParams(vmem_limit_bytes=VMEM_LIMIT),
        name=name,
    )(slots, *arrays, *tables)


def put(out_ref, *rows):
    out_ref[...] = jnp.concatenate(list(rows) + [jnp.zeros_like(rows[0])] * (8 - len(rows)), axis=0)


def write_near(x_best, x_sum, m_best, m_sum, own_ref, forth_ref, back_ref):
    put(own_ref, x_best[0], x_sum[0], x_best[1], x_sum[1], m_best[0], m_sum[0])
    put(back_ref, m_best[1], m_sum[1])
    put(forth_ref, m_best[2], m_sum[2])


def write_far(x_best, x_sum, m_best, m_sum, near, forth, back, out_ref):
    rows = [
        jnp.maximum(near[0:1], x_best[0]),
        near[1:2] + x_sum[0],
        jnp.maximum(near[4:5], jnp.maximum(forth[0:1], back[0:1])),
        near[5:6] + forth[1:2] + back[1:2],
        jnp.maximum(near[2:3], x_best[1]),
        near[3:4] + x_sum[1],
        x_best[2],
        x_sum[2],
        x_best[3],
        x_sum[3],
        m_best[0],
        m_sum[0],
        m_best[1],
        m_sum[1],
    ]
    out_ref[...] = jnp.concatenate(rows + [jnp.zeros_like(rows[0])] * 2, axis=0)


def sort_kernel(flags_ref, gathered_ref, home_ref, onward_ref, backward_ref):
    mid = flags_ref[0]
    worker = [flags_ref[1], flags_ref[2]]
    facing = [flags_ref[3], flags_ref[4]]

    def row(which, at):
        return gathered_ref[which, pl.ds(at, 1), :]

    def emit(ref, best0, best1, sum0, sum1):
        zero = jnp.zeros_like(best0)
        ref[...] = jnp.concatenate([best0, best1, sum0, sum1, zero, zero, zero, zero], axis=0)

    @pl.when(mid == 1)
    def _():
        emit(home_ref, row(worker[0], 2), row(worker[1], 2), row(worker[0], 3), row(worker[1], 3))
        emit(onward_ref, row(worker[0], 12), row(worker[1], 10), row(worker[0], 13), row(worker[1], 11))
        emit(backward_ref, row(worker[0], 10), row(worker[1], 12), row(worker[0], 11), row(worker[1], 13))

    @pl.when(mid == 0)
    def _():
        best = [jnp.maximum(row(worker[p], 0), row(facing[p], 4)) for p in range(2)]
        total = [row(worker[p], 1) + row(facing[p], 5) for p in range(2)]
        next_best = [jnp.maximum(row(worker[p], 6), row(facing[p], 8)) for p in range(2)]
        next_total = [row(worker[p], 7) + row(facing[p], 9) for p in range(2)]
        nothing = jnp.full_like(best[0], sentinel)
        none = jnp.zeros_like(best[0])
        emit(home_ref, best[0], best[1], total[0], total[1])
        emit(onward_ref, nothing, next_best[1], none, next_total[1])
        emit(backward_ref, next_best[0], nothing, next_total[0], none)


def sort(flags, gathered):
    tokens = gathered.shape[-1]
    vmem = pl.BlockSpec(memory_space=pltpu.VMEM)
    return pl.pallas_call(
        sort_kernel,
        in_specs=[pl.BlockSpec(memory_space=pltpu.SMEM), vmem],
        out_specs=[vmem] * 3,
        out_shape=[jax.ShapeDtypeStruct((8, tokens), jnp.float32)] * 3,
        name="sort_tables",
    )(flags, gathered)


def body(states, lengths):
    tokens = states.shape[2]
    candidates = lengths.shape[1]
    members = lax.axis_size("dev")
    group = lax.axis_index("grp")
    member = lax.axis_index("dev")
    mid = (group % 2) ^ (group // 2 % 2)
    prompt = 1 - mid
    direction = 2 * (group % 2) - 1

    def wanted(which, place):
        return prompt * candidates + which * members + (member + direction * place) % members

    m_group, c_group = group ^ (1 - mid), group ^ mid
    y_group = c_group ^ 3
    slots = [wanted(c_group, 0), wanted(y_group, 0), wanted(m_group, 0), wanted(m_group, -1), wanted(m_group, 1)]
    slots += [wanted(c_group, -1), wanted(y_group, 1), wanted(m_group, -2), wanted(m_group, 2)]
    order = [0, 1, 2, 3, 4, 0, 1, 5, 6, 7, 8]
    flat = lengths.reshape(1, -1)
    chosen = jnp.stack([slots[k] for k in order])[:, None] == lax.broadcasted_iota(jnp.int32, (1, flat.shape[1]), 1)
    slots = jnp.sum(jnp.where(chosen, flat, 0), axis=1)
    first, second = m_group % 4, (m_group ^ 1) % 4
    flags = jnp.stack([mid, first, second, first ^ 3, second ^ 3]).astype(jnp.int32)

    raw = states[:, 0]
    mid_flag = jnp.reshape(mid, (1,)).astype(jnp.int32)
    given = move(pick(mid_flag, raw), 0, 1)
    m_own, c_own = normalize(mid_flag, raw, given)

    c_next = move(c_own, 1)
    y_own = move(c_own, 0, 3)
    m_behind1 = move(m_own, 1)
    m_ahead1 = move(m_own, -1)
    payload, y_own = after(c_next, y_own)
    y_next = move(payload, 0, 3)
    m_behind2 = move(m_behind1, 1)
    m_ahead2 = move(m_ahead1, -1)

    near, forth, back = score(
        "near", [[0, 1]] * 3, slots, 0, [c_own, y_own], [m_own, m_behind1, m_ahead1], write_near, [], [8, 8, 8]
    )
    forth, back, m_ahead2 = after(forth, back, m_ahead2)
    forth = move(forth, 1)
    back = move(back, -1)
    (found,) = score(
        "far", [[0, 1, 3], [0, 1, 2]], slots, 5, [c_own, y_own, c_next, y_next], [m_behind2, m_ahead2],
        write_far, [near, forth, back], [16],
    )
    home, onward, backward = sort(flags, gather(found, 4))
    onward, backward = send_home(onward, 1), send_home(backward, -1)

    here = group * members + member
    columns = lax.broadcasted_iota(jnp.int32, lengths.shape, 1)
    own_lengths = jnp.sum(jnp.where(columns == here, lengths, 0), axis=1)
    best = jnp.maximum(home[:2], jnp.maximum(onward[:2], backward[:2]))
    total = home[2:4] + onward[2:4] + backward[2:4]
    token_valid = lax.broadcasted_iota(jnp.int32, (1, tokens), 1) < own_lengths[:, None]
    return (total[:, :1], jnp.where(token_valid, best, 0.0)[:, None, :])


def solution(mesh):
    in_specs = (P(None, ("grp", "dev"), None, None), P())
    out_specs = (P(None, ("grp", "dev")), P(None, ("grp", "dev"), None))
    return jax.shard_map(body, mesh=mesh, in_specs=in_specs, out_specs=out_specs, check_vma=False)
```

time: 360 us -> 110 us (0.31)
  the two profiles are of different devices: /device:TPU:1 before, /device:TPU:56 now
where the time goes in v2:
time: 110 us
  starting transfers between devices  50.3 us (46%)
  waiting for transfers between devices  34.9 us (32%)
  Pallas kernels  12.6 us (11%)
  blocking collectives  5.64 us (5%)
  local copies, waits for them, and re-layouts  3.51 us (3%)
  other arithmetic  1.71 us (2%)
    ppermute x10, starting transfers between devices, move(): return lax.ppermute(value, ('grp', 'dev'), pairs)  42.3 us
    ppermute x10, waiting for transfers between devices, move(): return lax.ppermute(value, ('grp', 'dev'), pairs)  28.2 us
    ppermute x2, starting transfers between devices, send_home(): return lax.ppermute(value, ('grp', 'dev'), pairs)  7.96 us
    pallas_call x2, Pallas kernels, score(): pl.pallas_call(functools.partial(score_kernel, plan, at, len(x_blocks), l...  7.55 us
    ppermute x2, waiting for transfers between devices, send_home(): return lax.ppermute(value, ('grp', 'dev'), pairs)  6.67 us
    all_gather x1, blocking collectives, gather(): lax.all_gather(value, 'grp', axis_index_groups=[list(range(g, g + size))...  5.64 us
    unnamed x10, local copies, waits for them, and re-layouts  2.84 us
    pallas_call x1, Pallas kernels, pick(): pl.pallas_call(pick_kernel, in_specs=[pl.BlockSpec(memory_space=pltpu.SME...  2.36 us
  transfers between devices with their start and end apart: 12, of which 6 were waited for; matrix products, arithmetic and copies ran while one was open for 1% of the time, Pallas kernels for 3%

profile of v2, /device:TPU:56, one launch (start us, length us, event | category | flops | bytes accessed | tf_op | source)
XLA Modules:
  0.0 109.6 jit_solution(18252561459636828184)
XLA Ops:
  0.7 2.4 %pick.1 = bf16[128,4096]{1,0:T(8,128)(2,1)} custom-call(s32[1]{0:T(128)} %bitcast.flags_ref, bf16[2,128,4096]{2,1,0:T(8,128)(2,1)} %bitcast.22), custom_call_target="tpu_custom_call" | custom-call | tf_op jit(solution)/shard_map/pick/pallas_call | solution.py:62
  3.1 1.9 %collective-permute-start = (bf16[128,4096]{1,0:T(8,128)(2,1)}, bf16[128,4096]{1,0:T(8,128)(2,1)S(1)}, u32[]{:S(2)}, u32[]{:S(2)}) collective-permute-start(bf16[128,4096]{1,0:T(8,128)(2,1)} %pick.1), channel_id=1, source_target_pairs={{0,32},{1,33},{2,34},{3,35},{4,36},{5,37},{6,38},{7,39},{8,40},{9,... | collective-permute-start | bytes 3145736 | tf_op jit(solution)/shard_map/ppermute | solution.py:40
  5.0 2.8 %collective-permute-done.given_ref = bf16[128,4096]{1,0:T(8,128)(2,1)S(1)} collective-permute-done((bf16[128,4096]{1,0:T(8,128)(2,1)}, bf16[128,4096]{1,0:T(8,128)(2,1)S(1)}, u32[]{:S(2)}, u32[]{:S(2)}) %collective-permute-start) | collective-permute-done | bytes 1048608 | tf_op jit(solution)/shard_map/ppermute | solution.py:40
  7.8 1.3 %normalize.1 = (bf16[128,4096]{1,0:T(8,128)(2,1)S(1)}, bf16[128,4096]{1,0:T(8,128)(2,1)S(1)}) custom-call(s32[1]{0:T(128)} %bitcast.flags_ref, bf16[2,128,4096]{2,1,0:T(8,128)(2,1)S(1)} %bitcast.23, bf16[128,4096]{1,0:T(8,128)(2,1)S(1)} %collective-permute-done.given_ref), custom_call_target="tpu_custom_call" | custom-call | tf_op jit(solution)/shard_map/normalize/pallas_call | solution.py:114
  9.1 3.8 %collective-permute-start.6 = (bf16[128,4096]{1,0:T(8,128)(2,1)S(1)}, bf16[128,4096]{1,0:T(8,128)(2,1)}, u32[]{:S(2)}, u32[]{:S(2)}) collective-permute-start(bf16[128,4096]{1,0:T(8,128)(2,1)S(1)} %get-tuple-element.18.refs_2_), channel_id=1, source_target_pairs={{0,1},{1,2},{2,3},{3,4},{4,5},{5,6},{6,7},{7,8},{8,9},{9,10},{10,1... | collective-permute-start | bytes 3145736 | tf_op jit(solution)/shard_map/ppermute | solution.py:40
  13.0 2.0 %collective-permute-start.1 = (bf16[128,4096]{1,0:T(8,128)(2,1)S(1)}, bf16[128,4096]{1,0:T(8,128)(2,1)S(1)}, u32[]{:S(2)}, u32[]{:S(2)}) collective-permute-start(bf16[128,4096]{1,0:T(8,128)(2,1)S(1)} %get-tuple-element.15.refs_0_), channel_id=1, source_target_pairs={{0,31},{1,0},{2,1},{3,2},{4,3},{5,4},{6,5},{7,6},{8,7},{9,8},{10,9... | collective-permute-start | bytes 3145736 | tf_op jit(solution)/shard_map/ppermute | solution.py:40
  15.0 2.0 %collective-permute-start.2 = (bf16[128,4096]{1,0:T(8,128)(2,1)S(1)}, bf16[128,4096]{1,0:T(8,128)(2,1)S(1)}, u32[]{:S(2)}, u32[]{:S(2)}) collective-permute-start(bf16[128,4096]{1,0:T(8,128)(2,1)S(1)} %get-tuple-element.15.refs_0_), channel_id=1, source_target_pairs={{0,96},{1,97},{2,98},{3,99},{4,100},{5,101},{6,102},{7,103},{8,104... | collective-permute-start | bytes 3145736 | tf_op jit(solution)/shard_map/ppermute | solution.py:40
  17.0 10.5 %collective-permute-start.4 = (bf16[128,4096]{1,0:T(8,128)(2,1)S(1)}, bf16[128,4096]{1,0:T(8,128)(2,1)}, u32[]{:S(2)}, u32[]{:S(2)}) collective-permute-start(bf16[128,4096]{1,0:T(8,128)(2,1)S(1)} %get-tuple-element.18.refs_2_), channel_id=1, source_target_pairs={{0,31},{1,0},{2,1},{3,2},{4,3},{5,4},{6,5},{7,6},{8,7},{9,8},{10,9... | collective-permute-start | bytes 3145736 | tf_op jit(solution)/shard_map/ppermute | solution.py:40
  27.6 1.0 copy-done.1
  28.6 6.8 %collective-permute-done.6.refs_4_ = bf16[128,4096]{1,0:T(8,128)(2,1)} collective-permute-done((bf16[128,4096]{1,0:T(8,128)(2,1)S(1)}, bf16[128,4096]{1,0:T(8,128)(2,1)}, u32[]{:S(2)}, u32[]{:S(2)}) %collective-permute-start.6) | collective-permute-done | bytes 1048608 | tf_op jit(solution)/shard_map/ppermute | solution.py:40
  35.4 4.5 %collective-permute-start.7 = (bf16[128,4096]{1,0:T(8,128)(2,1)}, bf16[128,4096]{1,0:T(8,128)(2,1)}, u32[]{:S(2)}, u32[]{:S(2)}) collective-permute-start(bf16[128,4096]{1,0:T(8,128)(2,1)} %collective-permute-done.6.refs_4_), channel_id=1, source_target_pairs={{0,1},{1,2},{2,3},{3,4},{4,5},{5,6},{6,7},{7,8},{8,9},{9,10},{10,1... | collective-permute-start | bytes 3145736 | tf_op jit(solution)/shard_map/ppermute | solution.py:40
  39.9 2.4 %collective-permute-done.2.refs_1_ = bf16[128,4096]{1,0:T(8,128)(2,1)S(1)} collective-permute-done((bf16[128,4096]{1,0:T(8,128)(2,1)S(1)}, bf16[128,4096]{1,0:T(8,128)(2,1)S(1)}, u32[]{:S(2)}, u32[]{:S(2)}) %collective-permute-start.2) | collective-permute-done | bytes 1048608 | tf_op jit(solution)/shard_map/ppermute | solution.py:40
  42.3 3.2 %collective-permute-start.3 = (bf16[128,4096]{1,0:T(8,128)(2,1)S(1)}, bf16[128,4096]{1,0:T(8,128)(2,1)}, u32[]{:S(2)}, u32[]{:S(2)}) collective-permute-start(bf16[128,4096]{1,0:T(8,128)(2,1)S(1)} %collective-permute-done.1.refs_2_), channel_id=1, source_target_pairs={{0,96},{1,97},{2,98},{3,99},{4,100},{5,101},{6,102},{7,103},{8,104... | collective-permute-start | bytes 3145736 | tf_op jit(solution)/shard_map/ppermute | solution.py:40
  45.5 13.2 %collective-permute-done.4.refs_3_ = bf16[128,4096]{1,0:T(8,128)(2,1)} collective-permute-done((bf16[128,4096]{1,0:T(8,128)(2,1)S(1)}, bf16[128,4096]{1,0:T(8,128)(2,1)}, u32[]{:S(2)}, u32[]{:S(2)}) %collective-permute-start.4) | collective-permute-done | bytes 1048608 | tf_op jit(solution)/shard_map/ppermute | solution.py:40
  58.7 5.8 %collective-permute-start.5 = (bf16[128,4096]{1,0:T(8,128)(2,1)}, bf16[128,4096]{1,0:T(8,128)(2,1)}, u32[]{:S(2)}, u32[]{:S(2)}) collective-permute-start(bf16[128,4096]{1,0:T(8,128)(2,1)} %collective-permute-done.4.refs_3_), channel_id=1, source_target_pairs={{0,31},{1,0},{2,1},{3,2},{4,3},{5,4},{6,5},{7,6},{8,7},{9,8},{10,9... | collective-permute-start | bytes 3145736 | tf_op jit(solution)/shard_map/ppermute | solution.py:40
  64.6 0.1 stack.65
  64.7 0.2 select_reduce_fusion.slots_ref
  64.9 1.2 %copy-done.2 = bf16[128,4096]{1,0:T(8,128)(2,1)S(1)} copy-done((bf16[128,4096]{1,0:T(8,128)(2,1)S(1)}, bf16[128,4096]{1,0:T(8,128)(2,1)}, u32[]{:S(2)}) %copy-start.2) | copy-done | bytes 1048600
  66.2 3.5 %near.1 = (f32[8,128]{1,0:T(8,128)S(1)}, f32[8,128]{1,0:T(8,128)S(1)}, f32[8,128]{1,0:T(8,128)S(1)}) custom-call(s32[11]{0:T(128)S(1)} %select_reduce_fusion.slots_ref, bf16[128,4096]{1,0:T(8,128)(2,1)S(1)} %get-tuple-element.15.refs_0_, bf16[128,4096]{1,0:T(8,128)(2,1)S(1)} %collective-permute-done.2.refs_1_, bf16[128,4096]{1,0:T(8,128)(2,1)S(1)} %copy-done.2, ...), custom_call_target="tpu_custom_call" | custom-call | flops 805306368 | bytes 5242880 | tf_op jit(solution)/shard_map/near/pallas_call | solution.py:193
  69.6 6.6 %collective-permute-start.8 = (f32[8,128]{1,0:T(8,128)S(1)}, f32[8,128]{1,0:T(8,128)S(1)}, u32[]{:S(2)}, u32[]{:S(2)}) collective-permute-start(f32[8,128]{1,0:T(8,128)S(1)} %get-tuple-element.23), channel_id=1, source_target_pairs={{0,31},{1,0},{2,1},{3,2},{4,3},{5,4},{6,5},{7,6},{8,7},{9,8},{10,9... | collective-permute-start | bytes 12296 | tf_op jit(solution)/shard_map/ppermute | solution.py:40
  76.2 1.9 %collective-permute-start.9 = (f32[8,128]{1,0:T(8,128)S(1)}, f32[8,128]{1,0:T(8,128)S(1)}, u32[]{:S(2)}, u32[]{:S(2)}) collective-permute-start(f32[8,128]{1,0:T(8,128)S(1)} %get-tuple-element.24), channel_id=1, source_target_pairs={{0,1},{1,2},{2,3},{3,4},{4,5},{5,6},{6,7},{7,8},{8,9},{9,10},{10,1... | collective-permute-start | bytes 12296 | tf_op jit(solution)/shard_map/ppermute | solution.py:40
  78.2 0.6 stack.55.flags_ref
  78.8 2.9 %collective-permute-done.9.refs_8_ = f32[8,128]{1,0:T(8,128)S(1)} collective-permute-done((f32[8,128]{1,0:T(8,128)S(1)}, f32[8,128]{1,0:T(8,128)S(1)}, u32[]{:S(2)}, u32[]{:S(2)}) %collective-permute-start.9) | collective-permute-done | bytes 4128 | tf_op jit(solution)/shard_map/ppermute | solution.py:40
  81.7 4.1 %far.1 = f32[16,128]{1,0:T(8,128)S(1)} custom-call(s32[11]{0:T(128)S(1)} %select_reduce_fusion.slots_ref, bf16[128,4096]{1,0:T(8,128)(2,1)S(1)} %get-tuple-element.15.refs_0_, bf16[128,4096]{1,0:T(8,128)(2,1)S(1)} %collective-permute-done.2.refs_1_, bf16[128,4096]{1,0:T(8,128)(2,1)S(1)} %collective-permute-done.1.refs_2_, ...), custom_call_target="tpu_custom_call" | custom-call | flops 1073741824 | bytes 6291456 | tf_op jit(solution)/shard_map/far/pallas_call | solution.py:193
  85.8 5.6 %all-gather = f32[64,128]{1,0:T(8,128)} all-gather(f32[16,128]{1,0:T(8,128)S(1)} %far.1), channel_id=2, replica_groups={{0,32,64,96},{128,160,192,224},{256,288,320,352},{384,416,448,480},{1,3..., dimensions={0}, use_global_device_ids=true | all-gather | bytes 40960 | tf_op jit(solution)/shard_map/all_gather | solution.py:45
  91.5 1.4 %sort_tables.1 = (f32[8,128]{1,0:T(8,128)}, f32[8,128]{1,0:T(8,128)}, f32[8,128]{1,0:T(8,128)}) custom-call(s32[5]{0:T(128)} %stack.55.flags_ref, f32[4,16,128]{2,1,0:T(8,128)} %bitcast.24), custom_call_target="tpu_custom_call" | custom-call | tf_op jit(solution)/shard_map/sort_tables/pallas_call | solution.py:279
  92.9 6.0 %collective-permute-start.10 = (f32[8,128]{1,0:T(8,128)}, f32[8,128]{1,0:T(8,128)S(1)}, u32[]{:S(2)}, u32[]{:S(2)}) collective-permute-start(f32[8,128]{1,0:T(8,128)} %get-tuple-element.26), channel_id=1, source_target_pairs={{0,1},{1,2},{2,3},{3,4},{4,5},{5,6},{6,7},{7,8},{8,9},{9,10},{10,1... | collective-permute-start | bytes 12296 | tf_op jit(solution)/shard_map/ppermute | solution.py:31
  98.9 1.9 %collective-permute-start.11 = (f32[8,128]{1,0:T(8,128)}, f32[8,128]{1,0:T(8,128)S(1)}, u32[]{:S(2)}, u32[]{:S(2)}) collective-permute-start(f32[8,128]{1,0:T(8,128)} %get-tuple-element.27), channel_id=1, source_target_pairs={{0,31},{1,0},{2,1},{3,2},{4,3},{5,4},{6,5},{7,6},{8,7},{9,8},{10,9... | collective-permute-start | bytes 12296 | tf_op jit(solution)/shard_map/ppermute | solution.py:31
  100.9 0.1 select_reduce_fusion.1
  101.0 6.7 %collective-permute-done.11 = f32[8,128]{1,0:T(8,128)S(1)} collective-permute-done((f32[8,128]{1,0:T(8,128)}, f32[8,128]{1,0:T(8,128)S(1)}, u32[]{:S(2)}, u32[]{:S(2)}) %collective-permute-start.11) | collective-permute-done | bytes 4128 | tf_op jit(solution)/shard_map/ppermute | solution.py:31
  107.6 1.4 %compare_select_fusion = (f32[2,128]{1,0:T(2,128)}, f32[2,128]{1,0:T(2,128)S(1)}) fusion(f32[8,128]{1,0:T(8,128)S(1)} %collective-permute-done.11, f32[8,128]{1,0:T(8,128)S(1)} %collective-permute-done.10, f32[8,128]{1,0:T(8,128)} %get-tuple-element.25, s32[2]{0:T(128)S(1)} %select_reduce_fusion.1), kind=kLoop, calls=%fused_computation.4 | loop fusion | flops 1536 | bytes 8200 | tf_op jit(solution)/shard_map/jit(_where)/select_n | solution.py:345
  109.0 0.6 copy.6
  (14 shorter events, 0.0 us)
Async XLA Ops:
  0.6 7.2 %copy-start = (bf16[2,1,128,4096]{3,2,1,0:T(8,128)(2,1)S(1)}, bf16[2,1,128,4096]{3,2,1,0:T(8,128)(2,1)}, u32[]{:S(2)}) copy-start(bf16[2,1,128,4096]{3,2,1,0:T(8,128)(2,1)} %param.2) | copy-start | bytes 6291460
  3.0 61.6 %copy-start.3 = (s32[2,512]{1,0:T(2,128)S(1)}, s32[2,512]{1,0:T(2,128)}, u32[]{:S(2)}) copy-start(s32[2,512]{1,0:T(2,128)} %param.3) | copy-start | bytes 12292
  3.1 4.8 %collective-permute-start = (bf16[128,4096]{1,0:T(8,128)(2,1)}, bf16[128,4096]{1,0:T(8,128)(2,1)S(1)}, u32[]{:S(2)}, u32[]{:S(2)}) collective-permute-start(bf16[128,4096]{1,0:T(8,128)(2,1)} %pick.1), channel_id=1, source_target_pairs={{0,32},{1,33},{2,34},{3,35},{4,36},{5,37},{6,38},{7,39},{8,40},{9,... | collective-permute-start | bytes 3145736 | tf_op jit(solution)/shard_map/ppermute | solution.py:40
  9.1 26.3 %collective-permute-start.6 = (bf16[128,4096]{1,0:T(8,128)(2,1)S(1)}, bf16[128,4096]{1,0:T(8,128)(2,1)}, u32[]{:S(2)}, u32[]{:S(2)}) collective-permute-start(bf16[128,4096]{1,0:T(8,128)(2,1)S(1)} %get-tuple-element.18.refs_2_), channel_id=1, source_target_pairs={{0,1},{1,2},{2,3},{3,4},{4,5},{5,6},{6,7},{7,8},{8,9},{9,10},{10,1... | collective-permute-start | bytes 3145736 | tf_op jit(solution)/shard_map/ppermute | solution.py:40
  13.0 26.9 %collective-permute-start.1 = (bf16[128,4096]{1,0:T(8,128)(2,1)S(1)}, bf16[128,4096]{1,0:T(8,128)(2,1)S(1)}, u32[]{:S(2)}, u32[]{:S(2)}) collective-permute-start(bf16[128,4096]{1,0:T(8,128)(2,1)S(1)} %get-tuple-element.15.refs_0_), channel_id=1, source_target_pairs={{0,31},{1,0},{2,1},{3,2},{4,3},{5,4},{6,5},{7,6},{8,7},{9,8},{10,9... | collective-permute-start | bytes 3145736 | tf_op jit(solution)/shard_map/ppermute | solution.py:40
  15.0 27.3 %collective-permute-start.2 = (bf16[128,4096]{1,0:T(8,128)(2,1)S(1)}, bf16[128,4096]{1,0:T(8,128)(2,1)S(1)}, u32[]{:S(2)}, u32[]{:S(2)}) collective-permute-start(bf16[128,4096]{1,0:T(8,128)(2,1)S(1)} %get-tuple-element.15.refs_0_), channel_id=1, source_target_pairs={{0,96},{1,97},{2,98},{3,99},{4,100},{5,101},{6,102},{7,103},{8,104... | collective-permute-start | bytes 3145736 | tf_op jit(solution)/shard_map/ppermute | solution.py:40
  17.0 41.7 %collective-permute-start.4 = (bf16[128,4096]{1,0:T(8,128)(2,1)S(1)}, bf16[128,4096]{1,0:T(8,128)(2,1)}, u32[]{:S(2)}, u32[]{:S(2)}) collective-permute-start(bf16[128,4096]{1,0:T(8,128)(2,1)S(1)} %get-tuple-element.18.refs_2_), channel_id=1, source_target_pairs={{0,31},{1,0},{2,1},{3,2},{4,3},{5,4},{6,5},{7,6},{8,7},{9,8},{10,9... | collective-permute-start | bytes 3145736 | tf_op jit(solution)/shard_map/ppermute | solution.py:40
  27.5 1.0 copy-start.1
  35.4 34.2 %collective-permute-start.7 = (bf16[128,4096]{1,0:T(8,128)(2,1)}, bf16[128,4096]{1,0:T(8,128)(2,1)}, u32[]{:S(2)}, u32[]{:S(2)}) collective-permute-start(bf16[128,4096]{1,0:T(8,128)(2,1)} %collective-permute-done.6.refs_4_), channel_id=1, source_target_pairs={{0,1},{1,2},{2,3},{3,4},{4,5},{5,6},{6,7},{7,8},{8,9},{9,10},{10,1... | collective-permute-start | bytes 3145736 | tf_op jit(solution)/shard_map/ppermute | solution.py:40
  42.3 36.5 %collective-permute-start.3 = (bf16[128,4096]{1,0:T(8,128)(2,1)S(1)}, bf16[128,4096]{1,0:T(8,128)(2,1)}, u32[]{:S(2)}, u32[]{:S(2)}) collective-permute-start(bf16[128,4096]{1,0:T(8,128)(2,1)S(1)} %collective-permute-done.1.refs_2_), channel_id=1, source_target_pairs={{0,96},{1,97},{2,98},{3,99},{4,100},{5,101},{6,102},{7,103},{8,104... | collective-permute-start | bytes 3145736 | tf_op jit(solution)/shard_map/ppermute | solution.py:40
  58.7 20.1 %collective-permute-start.5 = (bf16[128,4096]{1,0:T(8,128)(2,1)}, bf16[128,4096]{1,0:T(8,128)(2,1)}, u32[]{:S(2)}, u32[]{:S(2)}) collective-permute-start(bf16[128,4096]{1,0:T(8,128)(2,1)} %collective-permute-done.4.refs_3_), channel_id=1, source_target_pairs={{0,31},{1,0},{2,1},{3,2},{4,3},{5,4},{6,5},{7,6},{8,7},{9,8},{10,9... | collective-permute-start | bytes 3145736 | tf_op jit(solution)/shard_map/ppermute | solution.py:40
  64.9 1.2 %copy-start.2 = (bf16[128,4096]{1,0:T(8,128)(2,1)S(1)}, bf16[128,4096]{1,0:T(8,128)(2,1)}, u32[]{:S(2)}) copy-start(bf16[128,4096]{1,0:T(8,128)(2,1)} %copy-done.1) | copy-start | bytes 3145732
  69.6 9.2 %collective-permute-start.8 = (f32[8,128]{1,0:T(8,128)S(1)}, f32[8,128]{1,0:T(8,128)S(1)}, u32[]{:S(2)}, u32[]{:S(2)}) collective-permute-start(f32[8,128]{1,0:T(8,128)S(1)} %get-tuple-element.23), channel_id=1, source_target_pairs={{0,31},{1,0},{2,1},{3,2},{4,3},{5,4},{6,5},{7,6},{8,7},{9,8},{10,9... | collective-permute-start | bytes 12296 | tf_op jit(solution)/shard_map/ppermute | solution.py:40
  76.2 5.5 %collective-permute-start.9 = (f32[8,128]{1,0:T(8,128)S(1)}, f32[8,128]{1,0:T(8,128)S(1)}, u32[]{:S(2)}, u32[]{:S(2)}) collective-permute-start(f32[8,128]{1,0:T(8,128)S(1)} %get-tuple-element.24), channel_id=1, source_target_pairs={{0,1},{1,2},{2,3},{3,4},{4,5},{5,6},{6,7},{7,8},{8,9},{9,10},{10,1... | collective-permute-start | bytes 12296 | tf_op jit(solution)/shard_map/ppermute | solution.py:40
  92.9 8.1 %collective-permute-start.10 = (f32[8,128]{1,0:T(8,128)}, f32[8,128]{1,0:T(8,128)S(1)}, u32[]{:S(2)}, u32[]{:S(2)}) collective-permute-start(f32[8,128]{1,0:T(8,128)} %get-tuple-element.26), channel_id=1, source_target_pairs={{0,1},{1,2},{2,3},{3,4},{4,5},{5,6},{6,7},{7,8},{8,9},{9,10},{10,1... | collective-permute-start | bytes 12296 | tf_op jit(solution)/shard_map/ppermute | solution.py:31
  98.9 8.7 %collective-permute-start.11 = (f32[8,128]{1,0:T(8,128)}, f32[8,128]{1,0:T(8,128)S(1)}, u32[]{:S(2)}, u32[]{:S(2)}) collective-permute-start(f32[8,128]{1,0:T(8,128)} %get-tuple-element.27), channel_id=1, source_target_pairs={{0,31},{1,0},{2,1},{3,2},{4,3},{5,4},{6,5},{7,6},{8,7},{9,8},{10,9... | collective-permute-start | bytes 12296 | tf_op jit(solution)/shard_map/ppermute | solution.py:31

commit v3 on v2

v3 whole, which is shorter than its diff:
```python
import functools

import jax
import jax.numpy as jnp
from jax import lax
from jax.experimental import pallas as pl
from jax.experimental.pallas import tpu as pltpu
from jax.sharding import PartitionSpec as P


epsilon = 1e-06
sentinel = -4.0
VMEM_LIMIT = 24 * 1024 * 1024


def is_mid(g):
    return (g % 2) ^ (g // 2 % 2) == 1


def sign(g):
    return 2 * (g % 2) - 1


def move(value, mid, outer):
    groups, members = lax.axis_size("grp"), lax.axis_size("dev")
    pairs = []
    for g in range(groups):
        route = mid if is_mid(g) else outer
        if route is not None:
            by, mask = route
            for i in range(members):
                pairs.append((g * members + i, (g ^ mask) * members + (i + sign(g) * by) % members))
    return lax.ppermute(value, ("grp", "dev"), pairs)


def send_home(value, way):
    return move(value, (2 * way, 0), (-way, 0))


def gather(value, size):
    groups = lax.axis_size("grp")
    return lax.all_gather(
        value, "grp", axis_index_groups=[list(range(g, g + size)) for g in range(0, groups, size)]
    )


def after(value, *done):
    return lax.optimization_barrier((value, *done))


def normalize_kernel(flags_ref, states_ref, own_ref, given_ref, loaded, unit, load_sems, sems):
    steps = load_sems.shape[0]
    size = loaded.shape[1] // steps
    mid = flags_ref[0]

    def load(step):
        rows = pl.ds(step * size, size)
        return pltpu.make_async_copy(states_ref.at[:, rows], loaded.at[:, rows], load_sems.at[step])

    def stores(step):
        rows = pl.ds(step * size, size)
        return (
            pltpu.make_async_copy(unit.at[1 - mid, rows], own_ref.at[rows], sems.at[step, 0]),
            pltpu.make_async_copy(unit.at[mid, rows], given_ref.at[rows], sems.at[step, 1]),
        )

    for step in range(steps):
        load(step).start()
    for step in range(steps):
        load(step).wait()
        rows = pl.ds(step * size, size)
        for prompt in range(2):
            values = loaded[prompt, rows].astype(jnp.float32)
            total = jnp.sum(values * values, axis=-1, keepdims=True)
            unit[prompt, rows] = (values * lax.rsqrt(total + epsilon)).astype(jnp.bfloat16)
        for copy in stores(step):
            copy.start()
    for step in range(steps):
        for copy in stores(step):
            copy.wait()


def normalize(flags, states):
    _, tokens, width = states.shape
    steps = 4
    one = jax.ShapeDtypeStruct((tokens, width), jnp.bfloat16)
    hbm = pl.BlockSpec(memory_space=pltpu.HBM)
    return pl.pallas_call(
        normalize_kernel,
        in_specs=[pl.BlockSpec(memory_space=pltpu.SMEM), hbm],
        out_specs=[hbm] * 2,
        out_shape=[one, one],
        scratch_shapes=[
            pltpu.VMEM(states.shape, jnp.bfloat16),
            pltpu.VMEM(states.shape, jnp.bfloat16),
            pltpu.SemaphoreType.DMA((steps,)),
            pltpu.SemaphoreType.DMA((steps, 2)),
        ],
        compiler_params=pltpu.CompilerParams(vmem_limit_bytes=VMEM_LIMIT),
        name="normalize",
    )(flags, states)


def pair_stats(similarity, x_len, m_len):
    down = lax.broadcasted_iota(jnp.int32, similarity.shape, 0)
    lane = lax.broadcasted_iota(jnp.int32, (1, similarity.shape[1]), 1)
    x_best = jnp.max(jnp.where(down < m_len, similarity, sentinel), axis=0, keepdims=True)
    m_best = jnp.max(jnp.where(down < x_len, similarity.T, sentinel), axis=0, keepdims=True)
    x_sum = jnp.sum(jnp.where(lane < x_len, x_best, 0.0), axis=1, keepdims=True)
    m_sum = jnp.sum(jnp.where(lane < m_len, m_best, 0.0), axis=1, keepdims=True)
    x_count = jnp.full((1, 1), x_len, jnp.int32).astype(jnp.float32)
    m_count = jnp.full((1, 1), m_len, jnp.int32).astype(jnp.float32)
    score = 0.5 * (x_sum / x_count + m_sum / m_count)
    return x_best, m_best, jnp.broadcast_to(score, x_best.shape)


def score_kernel(plan, at, choice, x_count, m_count, array_count, out_count, assemble, flags_ref, slots_ref, *refs):
    sources = refs[:array_count]
    tables = refs[array_count : -3 - out_count]
    outs = refs[-3 - out_count : -3]
    x_stack, m_stack, sems = refs[-3:]
    tokens, width = sources[0].shape
    halves = sems.shape[1]
    size = width // halves

    def load(block, half, role):
        stack, row = (x_stack, block) if block < x_count else (m_stack, block - x_count)
        columns = pl.ds(half * size, size)
        return pltpu.make_async_copy(
            sources[choice[block][role]].at[:, columns],
            stack.at[pl.ds(row * tokens, tokens), columns],
            sems.at[block, half],
        )

    for role in range(2):

        @pl.when(flags_ref[0] == 1 - role)
        def _():
            for half in range(halves):
                for block in range(x_count + m_count):
                    load(block, half, role).start()

    similarity = None
    for half in range(halves):
        for block in range(x_count + m_count):
            load(block, half, 0).wait()
        columns = pl.ds(half * size, size)
        part = lax.dot_general(
            m_stack[:, columns], x_stack[:, columns], (((1,), (1,)), ((), ())),
            preferred_element_type=jnp.float32,
        )
        similarity = part if similarity is None else similarity + part
    x_best, x_sum = [None] * x_count, [None] * x_count
    m_best, m_sum = [None] * m_count, [None] * m_count

    def join(bests, totals, where, best, score):
        bests[where] = best if bests[where] is None else jnp.maximum(bests[where], best)
        totals[where] = score if totals[where] is None else totals[where] + score

    for m in range(m_count):
        for x in plan[m]:
            block = similarity[m * tokens : (m + 1) * tokens, x * tokens : (x + 1) * tokens]
            x_row, m_row, score = pair_stats(block, slots_ref[at + x], slots_ref[at + x_count + m])
            join(x_best, x_sum, x, x_row, score)
            join(m_best, m_sum, m, m_row, score)
    assemble(x_best, x_sum, m_best, m_sum, *tables, *outs)


def score(name, plan, flags, slots, at, arrays, x_choice, m_choice, assemble, tables, out_rows):
    tokens, width = arrays[0].shape
    x_count, m_count = len(x_choice), len(m_choice)
    vmem = pl.BlockSpec(memory_space=pltpu.VMEM)
    smem = pl.BlockSpec(memory_space=pltpu.SMEM)
    halves = 2
    kernel = functools.partial(
        score_kernel, plan, at, x_choice + m_choice, x_count, m_count, len(arrays), len(out_rows), assemble
    )
    return pl.pallas_call(
        kernel,
        in_specs=[smem] * 2 + [pl.BlockSpec(memory_space=pltpu.HBM)] * len(arrays) + [vmem] * len(tables),
        out_specs=[vmem for rows in out_rows],
        out_shape=[jax.ShapeDtypeStruct((rows, tokens), jnp.float32) for rows in out_rows],
        scratch_shapes=[
            pltpu.VMEM((x_count * tokens, width), jnp.bfloat16),
            pltpu.VMEM((m_count * tokens, width), jnp.bfloat16),
            pltpu.SemaphoreType.DMA((x_count + m_count, halves)),
        ],
        cost_estimate=pl.CostEstimate(
            flops=2 * x_count * m_count * tokens * tokens * width,
            bytes_accessed=2 * (x_count + m_count) * tokens * width,
            transcendentals=0,
        ),
        compiler_params=pltpu.CompilerParams(vmem_limit_bytes=VMEM_LIMIT),
        name=name,
    )(flags, slots, *arrays, *tables)


def put(out_ref, *rows):
    out_ref[...] = jnp.concatenate(list(rows) + [jnp.zeros_like(rows[0])] * (8 - len(rows)), axis=0)


def write_near(x_best, x_sum, m_best, m_sum, own_ref, forth_ref, back_ref):
    put(own_ref, x_best[0], x_sum[0], x_best[1], x_sum[1], m_best[0], m_sum[0])
    put(back_ref, m_best[1], m_sum[1])
    put(forth_ref, m_best[2], m_sum[2])


def write_far(x_best, x_sum, m_best, m_sum, near, forth, back, out_ref):
    rows = [
        jnp.maximum(near[0:1], x_best[0]),
        near[1:2] + x_sum[0],
        jnp.maximum(near[4:5], jnp.maximum(forth[0:1], back[0:1])),
        near[5:6] + forth[1:2] + back[1:2],
        jnp.maximum(near[2:3], x_best[1]),
        near[3:4] + x_sum[1],
        x_best[2],
        x_sum[2],
        x_best[3],
        x_sum[3],
        m_best[0],
        m_sum[0],
        m_best[1],
        m_sum[1],
    ]
    out_ref[...] = jnp.concatenate(rows + [jnp.zeros_like(rows[0])] * 2, axis=0)


def finish_kernel(slots_ref, here_ref, onward_ref, backward_ref, total_ref, best_ref):
    mid = slots_ref[13]
    worker = [slots_ref[14], slots_ref[15]]
    facing = [slots_ref[16], slots_ref[17]]
    lane = lax.broadcasted_iota(jnp.int32, (1, here_ref.shape[2]), 1)

    def join(parts):
        totals = []
        for prompt in range(2):
            best = [ref[which, pl.ds(at, 1), :] for ref, which, at in parts[prompt]]
            total = [ref[which, pl.ds(at + 1, 1), :] for ref, which, at in parts[prompt]]
            best = functools.reduce(jnp.maximum, best)
            best_ref[prompt] = jnp.where(lane < slots_ref[11 + prompt], best, 0.0)
            totals.append(sum(total[1:], total[0]))
        total_ref[...] = jnp.where(lane == 0, totals[0], totals[1])[:, :2]

    @pl.when(mid == 1)
    def _():
        join(
            [
                [(here_ref, worker[0], 2), (onward_ref, worker[0], 12), (backward_ref, worker[0], 10)],
                [(here_ref, worker[1], 2), (onward_ref, worker[1], 10), (backward_ref, worker[1], 12)],
            ]
        )

    @pl.when(mid == 0)
    def _():
        join(
            [
                [(ref, which, at) for ref, next_at in ((here_ref, 0), (neighbour, 6)) for which, at in
                 ((worker[prompt], next_at), (facing[prompt], next_at + (4 if next_at == 0 else 2)))]
                for prompt, neighbour in ((0, backward_ref), (1, onward_ref))
            ]
        )


def finish(slots, here, onward, backward):
    tokens = here.shape[-1]
    vmem = pl.BlockSpec(memory_space=pltpu.VMEM)
    smem = pl.BlockSpec(memory_space=pltpu.SMEM)
    return pl.pallas_call(
        finish_kernel,
        in_specs=[smem] + [vmem] * 3,
        out_specs=[vmem] * 2,
        out_shape=[jax.ShapeDtypeStruct((1, 2), jnp.float32), jax.ShapeDtypeStruct((2, 1, tokens), jnp.float32)],
        name="finish",
    )(slots, here, onward, backward)


def body(states, lengths):
    tokens = states.shape[2]
    candidates = lengths.shape[1]
    members = lax.axis_size("dev")
    group = lax.axis_index("grp")
    member = lax.axis_index("dev")
    mid = (group % 2) ^ (group // 2 % 2)
    prompt = 1 - mid
    direction = 2 * (group % 2) - 1

    def wanted(which, place):
        return prompt * candidates + which * members + (member + direction * place) % members

    m_group, c_group = group ^ (1 - mid), group ^ mid
    y_group = c_group ^ 3
    slots = [wanted(c_group, 0), wanted(y_group, 0), wanted(m_group, 0), wanted(m_group, -1), wanted(m_group, 1)]
    slots += [wanted(c_group, -1), wanted(y_group, 1), wanted(m_group, -2), wanted(m_group, 2)]
    order = [0, 1, 2, 3, 4, 0, 1, 5, 6, 7, 8]
    here = group * members + member
    wanted_slots = jnp.stack([slots[k] for k in order] + [here, candidates + here])
    flat = lengths.reshape(1, -1)
    chosen = wanted_slots[:, None] == lax.broadcasted_iota(jnp.int32, (1, flat.shape[1]), 1)
    first, second = m_group % 4, (m_group ^ 1) % 4
    slots = jnp.concatenate(
        [jnp.sum(jnp.where(chosen, flat, 0), axis=1), jnp.stack([mid, first, second, first ^ 3, second ^ 3])]
    )
    mid_flag = jnp.reshape(mid, (1,)).astype(jnp.int32)

    own, given = normalize(mid_flag, states[:, 0])
    other = move(given, (0, 1), (0, 1))
    a1 = move(own, (1, 0), (1, 0))
    b1 = move(own, (-1, 0), (0, 3))
    c1 = move(other, (1, 0), (-1, 0))
    d1 = move(other, (0, 3), (1, 0))
    a2 = move(a1, (1, 0), (0, 3))
    c2 = move(c1, (0, 3), (-1, 0))
    payload, d1 = after(b1, d1)
    b2 = move(payload, (-1, 0), None)
    d2 = move(d1, None, (1, 0))

    near, forth, back = score(
        "near", [[0, 1]] * 3, mid_flag, slots, 0, [own, other, a1, b1, c1, d1],
        [(1, 0), (5, 3)], [(0, 1), (2, 5), (3, 4)], write_near, [], [8, 8, 8],
    )
    forth, back, a2 = after(forth, back, a2)
    forth = move(forth, (1, 0), (1, 0))
    back = move(back, (-1, 0), (-1, 0))
    (found,) = score(
        "far", [[0, 1, 3], [0, 1, 2]], mid_flag, slots, 5, [own, other, a1, b1, c1, d1, a2, b2, c2, d2],
        [(1, 0), (5, 3), (4, 2), (8, 6)], [(6, 9), (7, 8)], write_far, [near, forth, back], [16],
    )
    found = gather(found, 4)
    total, best = finish(slots, found, send_home(found, 1), send_home(found, -1))
    return (total.reshape(2, 1), best)


def solution(mesh):
    in_specs = (P(None, ("grp", "dev"), None, None), P())
    out_specs = (P(None, ("grp", "dev")), P(None, ("grp", "dev"), None))
    return jax.shard_map(body, mesh=mesh, in_specs=in_specs, out_specs=out_specs, check_vma=False)
```

time: 110 us -> 106 us (0.964)
  the two profiles are of different devices: /device:TPU:56 before, /device:TPU:1 now
where the time goes in v3:
time: 106 us; the launch traced here: 105 us
  starting transfers between devices  47 us (44%)
  waiting for transfers between devices  30.2 us (28%)
  blocking collectives  13.5 us (13%)
  Pallas kernels  10.7 us (10%)
  local copies, waits for them, and re-layouts  2.39 us (2%)
    ppermute x13, starting transfers between devices, move(): return lax.ppermute(value, ('grp', 'dev'), pairs)  47 us
    ppermute x13, waiting for transfers between devices, move(): return lax.ppermute(value, ('grp', 'dev'), pairs)  30.2 us
    all_gather x1, blocking collectives, gather(): lax.all_gather(value, 'grp', axis_index_groups=[list(range(g, g + size))...  13.5 us
    pallas_call x2, Pallas kernels, score(): pl.pallas_call(kernel, in_specs=[smem] * 2 + [pl.BlockSpec(memory_space=p...  8.06 us
    unnamed x13, local copies, waits for them, and re-layouts  2.2 us
  transfers between devices with their start and end apart: 13, of which 7 were waited for; matrix products, arithmetic and copies ran while one was open for 0% of the time, Pallas kernels for 3%

profile of v3, /device:TPU:1, one launch (start us, length us, event | category | flops | bytes accessed | tf_op | source)
XLA Modules:
  0.0 105.0 jit_solution(4091438710956491841)
XLA Ops:
  0.7 1.6 %copy-done = bf16[2,1,128,4096]{3,2,1,0:T(8,128)(2,1)S(1)} copy-done((bf16[2,1,128,4096]{3,2,1,0:T(8,128)(2,1)S(1)}, bf16[2,1,128,4096]{3,2,1,0:T(8,128)(2,1)}, u32[]{:S(2)}) %copy-start) | copy-done | bytes 2097176
  2.3 1.3 %normalize.1 = (bf16[128,4096]{1,0:T(8,128)(2,1)S(1)}, bf16[128,4096]{1,0:T(8,128)(2,1)S(1)}) custom-call(s32[1]{0:T(128)} %bitcast.11.flags_ref, bf16[2,128,4096]{2,1,0:T(8,128)(2,1)S(1)} %bitcast.21), custom_call_target="tpu_custom_call" | custom-call | tf_op jit(solution)/shard_map/normalize/pallas_call | solution.py:88
  3.5 8.8 %collective-permute-start = (bf16[128,4096]{1,0:T(8,128)(2,1)S(1)}, bf16[128,4096]{1,0:T(8,128)(2,1)S(1)}, u32[]{:S(2)}, u32[]{:S(2)}) collective-permute-start(bf16[128,4096]{1,0:T(8,128)(2,1)S(1)} %get-tuple-element.15), channel_id=1, source_target_pairs={{0,32},{1,33},{2,34},{3,35},{4,36},{5,37},{6,38},{7,39},{8,40},{9,... | collective-permute-start | bytes 3145736 | tf_op jit(solution)/shard_map/ppermute | solution.py:33
  12.3 1.9 %collective-permute-start.1 = (bf16[128,4096]{1,0:T(8,128)(2,1)S(1)}, bf16[128,4096]{1,0:T(8,128)(2,1)S(1)}, u32[]{:S(2)}, u32[]{:S(2)}) collective-permute-start(bf16[128,4096]{1,0:T(8,128)(2,1)S(1)} %get-tuple-element.14.refs_0_), channel_id=1, source_target_pairs={{0,31},{1,0},{2,1},{3,2},{4,3},{5,4},{6,5},{7,6},{8,7},{9,8},{10,9... | collective-permute-start | bytes 3145736 | tf_op jit(solution)/shard_map/ppermute | solution.py:33
  14.3 6.7 %collective-permute-start.2 = (bf16[128,4096]{1,0:T(8,128)(2,1)S(1)}, bf16[128,4096]{1,0:T(8,128)(2,1)}, u32[]{:S(2)}, u32[]{:S(2)}) collective-permute-start(bf16[128,4096]{1,0:T(8,128)(2,1)S(1)} %get-tuple-element.14.refs_0_), channel_id=1, source_target_pairs={{0,96},{1,97},{2,98},{3,99},{4,100},{5,101},{6,102},{7,103},{8,104... | collective-permute-start | bytes 3145736 | tf_op jit(solution)/shard_map/ppermute | solution.py:33
  20.9 0.0 collective-permute-done.refs_1_
  21.0 3.4 %collective-permute-start.4 = (bf16[128,4096]{1,0:T(8,128)(2,1)S(1)}, bf16[128,4096]{1,0:T(8,128)(2,1)}, u32[]{:S(2)}, u32[]{:S(2)}) collective-permute-start(bf16[128,4096]{1,0:T(8,128)(2,1)S(1)} %collective-permute-done.refs_1_), channel_id=1, source_target_pairs={{0,31},{1,0},{2,1},{3,2},{4,3},{5,4},{6,5},{7,6},{8,7},{9,8},{10,9... | collective-permute-start | bytes 3145736 | tf_op jit(solution)/shard_map/ppermute | solution.py:33
  24.3 1.9 %collective-permute-start.3 = (bf16[128,4096]{1,0:T(8,128)(2,1)S(1)}, bf16[128,4096]{1,0:T(8,128)(2,1)}, u32[]{:S(2)}, u32[]{:S(2)}) collective-permute-start(bf16[128,4096]{1,0:T(8,128)(2,1)S(1)} %collective-permute-done.refs_1_), channel_id=1, source_target_pairs={{0,1},{1,2},{2,3},{3,4},{4,5},{5,6},{6,7},{7,8},{8,9},{9,10},{10,1... | collective-permute-start | bytes 3145736 | tf_op jit(solution)/shard_map/ppermute | solution.py:33
  26.3 4.9 %collective-permute-done.1.refs_2_ = bf16[128,4096]{1,0:T(8,128)(2,1)S(1)} collective-permute-done((bf16[128,4096]{1,0:T(8,128)(2,1)S(1)}, bf16[128,4096]{1,0:T(8,128)(2,1)S(1)}, u32[]{:S(2)}, u32[]{:S(2)}) %collective-permute-start.1) | collective-permute-done | bytes 1048608 | tf_op jit(solution)/shard_map/ppermute | solution.py:33
  31.2 1.9 %collective-permute-start.5 = (bf16[128,4096]{1,0:T(8,128)(2,1)S(1)}, bf16[128,4096]{1,0:T(8,128)(2,1)}, u32[]{:S(2)}, u32[]{:S(2)}) collective-permute-start(bf16[128,4096]{1,0:T(8,128)(2,1)S(1)} %collective-permute-done.1.refs_2_), channel_id=1, source_target_pairs={{0,96},{1,97},{2,98},{3,99},{4,100},{5,101},{6,102},{7,103},{8,104... | collective-permute-start | bytes 3145736 | tf_op jit(solution)/shard_map/ppermute | solution.py:33
  33.1 10.9 %collective-permute-done.2.refs_3_ = bf16[128,4096]{1,0:T(8,128)(2,1)} collective-permute-done((bf16[128,4096]{1,0:T(8,128)(2,1)S(1)}, bf16[128,4096]{1,0:T(8,128)(2,1)}, u32[]{:S(2)}, u32[]{:S(2)}) %collective-permute-start.2) | collective-permute-done | bytes 1048608 | tf_op jit(solution)/shard_map/ppermute | solution.py:33
  44.0 2.8 %collective-permute-done.4.refs_5_ = bf16[128,4096]{1,0:T(8,128)(2,1)} collective-permute-done((bf16[128,4096]{1,0:T(8,128)(2,1)S(1)}, bf16[128,4096]{1,0:T(8,128)(2,1)}, u32[]{:S(2)}, u32[]{:S(2)}) %collective-permute-start.4) | collective-permute-done | bytes 1048608 | tf_op jit(solution)/shard_map/ppermute | solution.py:33
  46.8 3.5 %collective-permute-start.6 = (bf16[128,4096]{1,0:T(8,128)(2,1)}, bf16[128,4096]{1,0:T(8,128)(2,1)}, u32[]{:S(2)}, u32[]{:S(2)}) collective-permute-start(bf16[128,4096]{1,0:T(8,128)(2,1)} %collective-permute-done.2.refs_3_), channel_id=1, source_target_pairs={{32,63},{33,32},{34,33},{35,34},{36,35},{37,36},{38,37},{39,38},{4... | collective-permute-start | bytes 3145736 | tf_op jit(solution)/shard_map/ppermute | solution.py:33
  50.3 1.6 %collective-permute-start.8 = (bf16[128,4096]{1,0:T(8,128)(2,1)}, bf16[128,4096]{1,0:T(8,128)(2,1)}, u32[]{:S(2)}, u32[]{:S(2)}) collective-permute-start(bf16[128,4096]{1,0:T(8,128)(2,1)} %collective-permute-done.4.refs_5_), channel_id=1, source_target_pairs={{0,31},{1,0},{2,1},{3,2},{4,3},{5,4},{6,5},{7,6},{8,7},{9,8},{10,9... | collective-permute-start | bytes 3145736 | tf_op jit(solution)/shard_map/ppermute | solution.py:33
  51.9 1.5 %collective-permute-done.3.refs_4_ = bf16[128,4096]{1,0:T(8,128)(2,1)} collective-permute-done((bf16[128,4096]{1,0:T(8,128)(2,1)S(1)}, bf16[128,4096]{1,0:T(8,128)(2,1)}, u32[]{:S(2)}, u32[]{:S(2)}) %collective-permute-start.3) | collective-permute-done | bytes 1048608 | tf_op jit(solution)/shard_map/ppermute | solution.py:33
  53.5 3.7 %collective-permute-start.7 = (bf16[128,4096]{1,0:T(8,128)(2,1)}, bf16[128,4096]{1,0:T(8,128)(2,1)}, u32[]{:S(2)}, u32[]{:S(2)}) collective-permute-start(bf16[128,4096]{1,0:T(8,128)(2,1)} %collective-permute-done.3.refs_4_), channel_id=1, source_target_pairs={{0,1},{1,2},{2,3},{3,4},{4,5},{5,6},{6,7},{7,8},{8,9},{9,10},{10,1... | collective-permute-start | bytes 3145736 | tf_op jit(solution)/shard_map/ppermute | solution.py:33
  57.3 0.1 stack.64
  57.4 0.2 select_reduce_fusion
  57.6 0.1 concatenate.3.slots_ref
  57.7 3.4 %near.1 = (f32[8,128]{1,0:T(8,128)S(1)}, f32[8,128]{1,0:T(8,128)S(1)}, f32[8,128]{1,0:T(8,128)S(1)}) custom-call(s32[1]{0:T(128)} %bitcast.11.flags_ref, s32[18]{0:T(128)S(1)} %concatenate.3.slots_ref, bf16[128,4096]{1,0:T(8,128)(2,1)S(1)} %get-tuple-element.14.refs_0_, bf16[128,4096]{1,0:T(8,128)(2,1)S(1)} %collective-permute-done.refs_1_, ...), custom_call_target="tpu_custom_call" | custom-call | flops 805306368 | bytes 5242880 | tf_op jit(solution)/shard_map/near/pallas_call | solution.py:178
  61.1 3.9 %collective-permute-done.5.refs_6_ = bf16[128,4096]{1,0:T(8,128)(2,1)} collective-permute-done((bf16[128,4096]{1,0:T(8,128)(2,1)S(1)}, bf16[128,4096]{1,0:T(8,128)(2,1)}, u32[]{:S(2)}, u32[]{:S(2)}) %collective-permute-start.5) | collective-permute-done | bytes 1048608 | tf_op jit(solution)/shard_map/ppermute | solution.py:33
  65.0 3.4 %collective-permute-start.10 = (f32[8,128]{1,0:T(8,128)S(1)}, f32[8,128]{1,0:T(8,128)S(1)}, u32[]{:S(2)}, u32[]{:S(2)}) collective-permute-start(f32[8,128]{1,0:T(8,128)S(1)} %get-tuple-element.23), channel_id=1, source_target_pairs={{0,1},{1,2},{2,3},{3,4},{4,5},{5,6},{6,7},{7,8},{8,9},{9,10},{10,1... | collective-permute-start | bytes 12296 | tf_op jit(solution)/shard_map/ppermute | solution.py:33
  68.4 1.9 %collective-permute-start.9 = (f32[8,128]{1,0:T(8,128)S(1)}, f32[8,128]{1,0:T(8,128)S(1)}, u32[]{:S(2)}, u32[]{:S(2)}) collective-permute-start(f32[8,128]{1,0:T(8,128)S(1)} %get-tuple-element.22), channel_id=1, source_target_pairs={{0,31},{1,0},{2,1},{3,2},{4,3},{5,4},{6,5},{7,6},{8,7},{9,8},{10,9... | collective-permute-start | bytes 12296 | tf_op jit(solution)/shard_map/ppermute | solution.py:33
  70.3 0.0 collective-permute-done.10.refs_12_
  70.3 5.0 %collective-permute-done.9.refs_11_ = f32[8,128]{1,0:T(8,128)S(1)} collective-permute-done((f32[8,128]{1,0:T(8,128)S(1)}, f32[8,128]{1,0:T(8,128)S(1)}, u32[]{:S(2)}, u32[]{:S(2)}) %collective-permute-start.9) | collective-permute-done | bytes 4128 | tf_op jit(solution)/shard_map/ppermute | solution.py:33
  75.3 4.6 %far.1 = f32[16,128]{1,0:T(8,128)S(1)} custom-call(s32[1]{0:T(128)} %bitcast.11.flags_ref, s32[18]{0:T(128)S(1)} %concatenate.3.slots_ref, bf16[128,4096]{1,0:T(8,128)(2,1)S(1)} %get-tuple-element.14.refs_0_, bf16[128,4096]{1,0:T(8,128)(2,1)S(1)} %collective-permute-done.refs_1_, bf16[128,4096]{1,0:T(8,128)(2,1)S(1)} %collective-permute-done.1.refs_2_, ...), custom_call_target="tpu_custom_call" | custom-call | flops 1073741824 | bytes 6291456 | tf_op jit(solution)/shard_map/far/pallas_call | solution.py:178
  80.0 13.5 %all-gather = f32[64,128]{1,0:T(8,128)S(1)} all-gather(f32[16,128]{1,0:T(8,128)S(1)} %far.1), channel_id=2, replica_groups={{0,32,64,96},{128,160,192,224},{256,288,320,352},{384,416,448,480},{1,3..., dimensions={0}, use_global_device_ids=true | all-gather | bytes 40960 | tf_op jit(solution)/shard_map/all_gather | solution.py:42
  93.5 1.9 %collective-permute-start.11 = (f32[4,16,128]{2,1,0:T(8,128)S(1)}, f32[4,16,128]{2,1,0:T(8,128)S(1)}, u32[]{:S(2)}, u32[]{:S(2)}) collective-permute-start(f32[4,16,128]{2,1,0:T(8,128)S(1)} %bitcast.22), channel_id=1, source_target_pairs={{0,1},{1,2},{2,3},{3,4},{4,5},{5,6},{6,7},{7,8},{8,9},{9,10},{10,1... | collective-permute-start | bytes 98312 | tf_op jit(solution)/shard_map/ppermute | solution.py:33
  95.4 6.4 %collective-permute-start.12 = (f32[4,16,128]{2,1,0:T(8,128)S(1)}, f32[4,16,128]{2,1,0:T(8,128)S(1)}, u32[]{:S(2)}, u32[]{:S(2)}) collective-permute-start(f32[4,16,128]{2,1,0:T(8,128)S(1)} %bitcast.23), channel_id=1, source_target_pairs={{0,31},{1,0},{2,1},{3,2},{4,3},{5,4},{6,5},{7,6},{8,7},{9,8},{10,9... | collective-permute-start | bytes 98312 | tf_op jit(solution)/shard_map/ppermute | solution.py:33
  101.8 1.1 %collective-permute-done.12.backward_ref = f32[4,16,128]{2,1,0:T(8,128)S(1)} collective-permute-done((f32[4,16,128]{2,1,0:T(8,128)S(1)}, f32[4,16,128]{2,1,0:T(8,128)S(1)}, u32[]{:S(2)}, u32[]{:S(2)}) %collective-permute-start.12) | collective-permute-done | bytes 32800 | tf_op jit(solution)/shard_map/ppermute | solution.py:33
  103.0 0.6 copy-done.4
  103.6 1.4 %finish.1 = (f32[1,2]{1,0:T(1,128)}, f32[2,1,128]{2,1,0:T(1,128)}) custom-call(s32[18]{0:T(128)} %copy-done.1, f32[4,16,128]{2,1,0:T(8,128)} %bitcast.24, f32[4,16,128]{2,1,0:T(8,128)} %copy-done.3, f32[4,16,128]{2,1,0:T(8,128)} %copy-done.4), custom_call_target="tpu_custom_call" | custom-call | tf_op jit(solution)/shard_map/finish/pallas_call | solution.py:268
  (15 shorter events, 0.0 us)
Async XLA Ops:
  0.6 56.7 %copy-start.5 = (s32[2,512]{1,0:T(2,128)S(1)}, s32[2,512]{1,0:T(2,128)}, u32[]{:S(2)}) copy-start(s32[2,512]{1,0:T(2,128)} %param.3) | copy-start | bytes 12292
  0.7 1.6 %copy-start = (bf16[2,1,128,4096]{3,2,1,0:T(8,128)(2,1)S(1)}, bf16[2,1,128,4096]{3,2,1,0:T(8,128)(2,1)}, u32[]{:S(2)}) copy-start(bf16[2,1,128,4096]{3,2,1,0:T(8,128)(2,1)} %param.2) | copy-start | bytes 6291460
  3.5 17.4 %collective-permute-start = (bf16[128,4096]{1,0:T(8,128)(2,1)S(1)}, bf16[128,4096]{1,0:T(8,128)(2,1)S(1)}, u32[]{:S(2)}, u32[]{:S(2)}) collective-permute-start(bf16[128,4096]{1,0:T(8,128)(2,1)S(1)} %get-tuple-element.15), channel_id=1, source_target_pairs={{0,32},{1,33},{2,34},{3,35},{4,36},{5,37},{6,38},{7,39},{8,40},{9,... | collective-permute-start | bytes 3145736 | tf_op jit(solution)/shard_map/ppermute | solution.py:33
  12.3 18.9 %collective-permute-start.1 = (bf16[128,4096]{1,0:T(8,128)(2,1)S(1)}, bf16[128,4096]{1,0:T(8,128)(2,1)S(1)}, u32[]{:S(2)}, u32[]{:S(2)}) collective-permute-start(bf16[128,4096]{1,0:T(8,128)(2,1)S(1)} %get-tuple-element.14.refs_0_), channel_id=1, source_target_pairs={{0,31},{1,0},{2,1},{3,2},{4,3},{5,4},{6,5},{7,6},{8,7},{9,8},{10,9... | collective-permute-start | bytes 3145736 | tf_op jit(solution)/shard_map/ppermute | solution.py:33
  14.3 29.7 %collective-permute-start.2 = (bf16[128,4096]{1,0:T(8,128)(2,1)S(1)}, bf16[128,4096]{1,0:T(8,128)(2,1)}, u32[]{:S(2)}, u32[]{:S(2)}) collective-permute-start(bf16[128,4096]{1,0:T(8,128)(2,1)S(1)} %get-tuple-element.14.refs_0_), channel_id=1, source_target_pairs={{0,96},{1,97},{2,98},{3,99},{4,100},{5,101},{6,102},{7,103},{8,104... | collective-permute-start | bytes 3145736 | tf_op jit(solution)/shard_map/ppermute | solution.py:33
  21.0 25.8 %collective-permute-start.4 = (bf16[128,4096]{1,0:T(8,128)(2,1)S(1)}, bf16[128,4096]{1,0:T(8,128)(2,1)}, u32[]{:S(2)}, u32[]{:S(2)}) collective-permute-start(bf16[128,4096]{1,0:T(8,128)(2,1)S(1)} %collective-permute-done.refs_1_), channel_id=1, source_target_pairs={{0,31},{1,0},{2,1},{3,2},{4,3},{5,4},{6,5},{7,6},{8,7},{9,8},{10,9... | collective-permute-start | bytes 3145736 | tf_op jit(solution)/shard_map/ppermute | solution.py:33
  24.3 29.1 %collective-permute-start.3 = (bf16[128,4096]{1,0:T(8,128)(2,1)S(1)}, bf16[128,4096]{1,0:T(8,128)(2,1)}, u32[]{:S(2)}, u32[]{:S(2)}) collective-permute-start(bf16[128,4096]{1,0:T(8,128)(2,1)S(1)} %collective-permute-done.refs_1_), channel_id=1, source_target_pairs={{0,1},{1,2},{2,3},{3,4},{4,5},{5,6},{6,7},{7,8},{8,9},{9,10},{10,1... | collective-permute-start | bytes 3145736 | tf_op jit(solution)/shard_map/ppermute | solution.py:33
  31.2 33.8 %collective-permute-start.5 = (bf16[128,4096]{1,0:T(8,128)(2,1)S(1)}, bf16[128,4096]{1,0:T(8,128)(2,1)}, u32[]{:S(2)}, u32[]{:S(2)}) collective-permute-start(bf16[128,4096]{1,0:T(8,128)(2,1)S(1)} %collective-permute-done.1.refs_2_), channel_id=1, source_target_pairs={{0,96},{1,97},{2,98},{3,99},{4,100},{5,101},{6,102},{7,103},{8,104... | collective-permute-start | bytes 3145736 | tf_op jit(solution)/shard_map/ppermute | solution.py:33
  46.8 28.6 %collective-permute-start.6 = (bf16[128,4096]{1,0:T(8,128)(2,1)}, bf16[128,4096]{1,0:T(8,128)(2,1)}, u32[]{:S(2)}, u32[]{:S(2)}) collective-permute-start(bf16[128,4096]{1,0:T(8,128)(2,1)} %collective-permute-done.2.refs_3_), channel_id=1, source_target_pairs={{32,63},{33,32},{34,33},{35,34},{36,35},{37,36},{38,37},{39,38},{4... | collective-permute-start | bytes 3145736 | tf_op jit(solution)/shard_map/ppermute | solution.py:33
  50.3 25.0 %collective-permute-start.8 = (bf16[128,4096]{1,0:T(8,128)(2,1)}, bf16[128,4096]{1,0:T(8,128)(2,1)}, u32[]{:S(2)}, u32[]{:S(2)}) collective-permute-start(bf16[128,4096]{1,0:T(8,128)(2,1)} %collective-permute-done.4.refs_5_), channel_id=1, source_target_pairs={{0,31},{1,0},{2,1},{3,2},{4,3},{5,4},{6,5},{7,6},{8,7},{9,8},{10,9... | collective-permute-start | bytes 3145736 | tf_op jit(solution)/shard_map/ppermute | solution.py:33
  53.5 21.9 %collective-permute-start.7 = (bf16[128,4096]{1,0:T(8,128)(2,1)}, bf16[128,4096]{1,0:T(8,128)(2,1)}, u32[]{:S(2)}, u32[]{:S(2)}) collective-permute-start(bf16[128,4096]{1,0:T(8,128)(2,1)} %collective-permute-done.3.refs_4_), channel_id=1, source_target_pairs={{0,1},{1,2},{2,3},{3,4},{4,5},{5,6},{6,7},{7,8},{8,9},{9,10},{10,1... | collective-permute-start | bytes 3145736 | tf_op jit(solution)/shard_map/ppermute | solution.py:33
  57.7 17.6 %copy-start.1 = (s32[18]{0:T(128)}, s32[18]{0:T(128)S(1)}, u32[]{:S(2)}) copy-start(s32[18]{0:T(128)S(1)} %concatenate.3.slots_ref) | copy-start | bytes 220
  65.0 5.3 %collective-permute-start.10 = (f32[8,128]{1,0:T(8,128)S(1)}, f32[8,128]{1,0:T(8,128)S(1)}, u32[]{:S(2)}, u32[]{:S(2)}) collective-permute-start(f32[8,128]{1,0:T(8,128)S(1)} %get-tuple-element.23), channel_id=1, source_target_pairs={{0,1},{1,2},{2,3},{3,4},{4,5},{5,6},{6,7},{7,8},{8,9},{9,10},{10,1... | collective-permute-start | bytes 12296 | tf_op jit(solution)/shard_map/ppermute | solution.py:33
  68.4 7.0 %collective-permute-start.9 = (f32[8,128]{1,0:T(8,128)S(1)}, f32[8,128]{1,0:T(8,128)S(1)}, u32[]{:S(2)}, u32[]{:S(2)}) collective-permute-start(f32[8,128]{1,0:T(8,128)S(1)} %get-tuple-element.22), channel_id=1, source_target_pairs={{0,31},{1,0},{2,1},{3,2},{4,3},{5,4},{6,5},{7,6},{8,7},{9,8},{10,9... | collective-permute-start | bytes 12296 | tf_op jit(solution)/shard_map/ppermute | solution.py:33
  93.5 9.5 %copy-start.2 = (f32[64,128]{1,0:T(8,128)}, f32[64,128]{1,0:T(8,128)S(1)}, u32[]{:S(2)}) copy-start(f32[64,128]{1,0:T(8,128)S(1)} %all-gather) | copy-start | bytes 98308
  93.5 8.3 %collective-permute-start.11 = (f32[4,16,128]{2,1,0:T(8,128)S(1)}, f32[4,16,128]{2,1,0:T(8,128)S(1)}, u32[]{:S(2)}, u32[]{:S(2)}) collective-permute-start(f32[4,16,128]{2,1,0:T(8,128)S(1)} %bitcast.22), channel_id=1, source_target_pairs={{0,1},{1,2},{2,3},{3,4},{4,5},{5,6},{6,7},{7,8},{8,9},{9,10},{10,1... | collective-permute-start | bytes 98312 | tf_op jit(solution)/shard_map/ppermute | solution.py:33
  95.4 7.5 %collective-permute-start.12 = (f32[4,16,128]{2,1,0:T(8,128)S(1)}, f32[4,16,128]{2,1,0:T(8,128)S(1)}, u32[]{:S(2)}, u32[]{:S(2)}) collective-permute-start(f32[4,16,128]{2,1,0:T(8,128)S(1)} %bitcast.23), channel_id=1, source_target_pairs={{0,31},{1,0},{2,1},{3,2},{4,3},{5,4},{6,5},{7,6},{8,7},{9,8},{10,9... | collective-permute-start | bytes 98312 | tf_op jit(solution)/shard_map/ppermute | solution.py:33
  101.8 1.1 %copy-start.3 = (f32[4,16,128]{2,1,0:T(8,128)}, f32[4,16,128]{2,1,0:T(8,128)S(1)}, u32[]{:S(2)}) copy-start(f32[4,16,128]{2,1,0:T(8,128)S(1)} %collective-permute-done.11.onward_ref) | copy-start | bytes 98308
  103.0 0.6 copy-start.4

commit v4 on v3

--- a/solution.py
+++ b/solution.py
@@ -166,7 +166,7 @@
     assemble(x_best, x_sum, m_best, m_sum, *tables, *outs)
 
 
-def score(name, plan, flags, slots, at, arrays, x_choice, m_choice, assemble, tables, out_rows):
+def score(name, plan, flags, slots, at, arrays, x_choice, m_choice, assemble, tables, out_rows, weight=1):
     tokens, width = arrays[0].shape
     x_count, m_count = len(x_choice), len(m_choice)
     vmem = pl.BlockSpec(memory_space=pltpu.VMEM)
@@ -186,8 +186,8 @@
             pltpu.SemaphoreType.DMA((x_count + m_count, halves)),
         ],
         cost_estimate=pl.CostEstimate(
-            flops=2 * x_count * m_count * tokens * tokens * width,
-            bytes_accessed=2 * (x_count + m_count) * tokens * width,
+            flops=weight * 2 * x_count * m_count * tokens * tokens * width,
+            bytes_accessed=weight * 2 * (x_count + m_count) * tokens * width,
             transcendentals=0,
         ),
         compiler_params=pltpu.CompilerParams(vmem_limit_bytes=VMEM_LIMIT),
@@ -205,12 +205,12 @@
     put(forth_ref, m_best[2], m_sum[2])
 
 
-def write_far(x_best, x_sum, m_best, m_sum, near, forth, back, out_ref):
+def write_far(x_best, x_sum, m_best, m_sum, near, out_ref):
     rows = [
         jnp.maximum(near[0:1], x_best[0]),
         near[1:2] + x_sum[0],
-        jnp.maximum(near[4:5], jnp.maximum(forth[0:1], back[0:1])),
-        near[5:6] + forth[1:2] + back[1:2],
+        near[4:5],
+        near[5:6],
         jnp.maximum(near[2:3], x_best[1]),
         near[3:4] + x_sum[1],
         x_best[2],
@@ -316,16 +316,19 @@
 
     near, forth, back = score(
         "near", [[0, 1]] * 3, mid_flag, slots, 0, [own, other, a1, b1, c1, d1],
-        [(1, 0), (5, 3)], [(0, 1), (2, 5), (3, 4)], write_near, [], [8, 8, 8],
+        [(1, 0), (5, 3)], [(0, 1), (2, 5), (3, 4)], write_near, [], [8, 8, 8], 10,
     )
     forth, back, a2 = after(forth, back, a2)
     forth = move(forth, (1, 0), (1, 0))
     back = move(back, (-1, 0), (-1, 0))
     (found,) = score(
-        "far", [[0, 1, 3], [0, 1, 2]], mid_flag, slots, 5, [own, other, a1, b1, c1, d1, a2, b2, c2, d2],
-        [(1, 0), (5, 3), (4, 2), (8, 6)], [(6, 9), (7, 8)], write_far, [near, forth, back], [16],
-    )
-    found = gather(found, 4)
+        "far", [[0, 1, 3], [0, 1, 2]], mid_flag, slots, 5, [own, other, a1, b1, c1, d1, d2, b2, c2, a2],
+        [(1, 0), (5, 3), (4, 2), (8, 9)], [(9, 6), (7, 8)], write_far, [near], [16],
+    )
+    row = lax.broadcasted_iota(jnp.int32, (found.shape[0], 1), 0)
+    best = jnp.maximum(found, jnp.maximum(forth[:1], back[:1]))
+    total = found + forth[1:2] + back[1:2]
+    found = gather(jnp.where(row == 2, best, jnp.where(row == 3, total, found)), 4)
     total, best = finish(slots, found, send_home(found, 1), send_home(found, -1))
     return (total.reshape(2, 1), best)
 

time: 106 us -> 103 us (0.972)
  blocking collectives: 13.5 us -> 11.9 us
    all_gather x1, blocking collectives: 13.5 us -> 11.9 us  [gather(): lax.all_gather(value, 'grp', axis_index_groups=[list(range(g, g + size))...]
where the time goes in v4:
time: 103 us
  starting transfers between devices  46.1 us (45%)
  waiting for transfers between devices  31 us (30%)
  blocking collectives  11.9 us (12%)
  Pallas kernels  10.1 us (10%)
  local copies, waits for them, and re-layouts  2.39 us (2%)
  between operations  1.04 us (1%)
    ppermute x13, starting transfers between devices, move(): return lax.ppermute(value, ('grp', 'dev'), pairs)  46.1 us
    ppermute x13, waiting for transfers between devices, move(): return lax.ppermute(value, ('grp', 'dev'), pairs)  31 us
    all_gather x1, blocking collectives, gather(): lax.all_gather(value, 'grp', axis_index_groups=[list(range(g, g + size))...  11.9 us
    pallas_call x2, Pallas kernels, score(): pl.pallas_call(kernel, in_specs=[smem] * 2 + [pl.BlockSpec(memory_space=p...  7.45 us
    unnamed x13, local copies, waits for them, and re-layouts  2.2 us
  transfers between devices with their start and end apart: 13, of which 7 were waited for; matrix products, arithmetic and copies ran while one was open for 0% of the time, Pallas kernels for 3%

profile of v4, /device:TPU:1, one launch (start us, length us, event | category | flops | bytes accessed | tf_op | source)
XLA Modules:
  0.0 102.7 jit_solution(2479629932415718040)
XLA Ops:
  0.7 1.6 %copy-done = bf16[2,1,128,4096]{3,2,1,0:T(8,128)(2,1)S(1)} copy-done((bf16[2,1,128,4096]{3,2,1,0:T(8,128)(2,1)S(1)}, bf16[2,1,128,4096]{3,2,1,0:T(8,128)(2,1)}, u32[]{:S(2)}) %copy-start) | copy-done | bytes 2097176
  2.3 1.3 %normalize.1 = (bf16[128,4096]{1,0:T(8,128)(2,1)S(1)}, bf16[128,4096]{1,0:T(8,128)(2,1)S(1)}) custom-call(s32[1]{0:T(128)} %bitcast.11.flags_ref, bf16[2,128,4096]{2,1,0:T(8,128)(2,1)S(1)} %bitcast.27), custom_call_target="tpu_custom_call" | custom-call | tf_op jit(solution)/shard_map/normalize/pallas_call | solution.py:88
  3.5 8.8 %collective-permute-start = (bf16[128,4096]{1,0:T(8,128)(2,1)S(1)}, bf16[128,4096]{1,0:T(8,128)(2,1)S(1)}, u32[]{:S(2)}, u32[]{:S(2)}) collective-permute-start(bf16[128,4096]{1,0:T(8,128)(2,1)S(1)} %get-tuple-element.15), channel_id=1, source_target_pairs={{0,32},{1,33},{2,34},{3,35},{4,36},{5,37},{6,38},{7,39},{8,40},{9,... | collective-permute-start | bytes 3145736 | tf_op jit(solution)/shard_map/ppermute | solution.py:33
  12.3 1.9 %collective-permute-start.1 = (bf16[128,4096]{1,0:T(8,128)(2,1)S(1)}, bf16[128,4096]{1,0:T(8,128)(2,1)S(1)}, u32[]{:S(2)}, u32[]{:S(2)}) collective-permute-start(bf16[128,4096]{1,0:T(8,128)(2,1)S(1)} %get-tuple-element.14.refs_0_), channel_id=1, source_target_pairs={{0,31},{1,0},{2,1},{3,2},{4,3},{5,4},{6,5},{7,6},{8,7},{9,8},{10,9... | collective-permute-start | bytes 3145736 | tf_op jit(solution)/shard_map/ppermute | solution.py:33
  14.3 6.7 %collective-permute-start.2 = (bf16[128,4096]{1,0:T(8,128)(2,1)S(1)}, bf16[128,4096]{1,0:T(8,128)(2,1)}, u32[]{:S(2)}, u32[]{:S(2)}) collective-permute-start(bf16[128,4096]{1,0:T(8,128)(2,1)S(1)} %get-tuple-element.14.refs_0_), channel_id=1, source_target_pairs={{0,96},{1,97},{2,98},{3,99},{4,100},{5,101},{6,102},{7,103},{8,104... | collective-permute-start | bytes 3145736 | tf_op jit(solution)/shard_map/ppermute | solution.py:33
  20.9 0.0 collective-permute-done.refs_1_
  21.0 3.4 %collective-permute-start.4 = (bf16[128,4096]{1,0:T(8,128)(2,1)S(1)}, bf16[128,4096]{1,0:T(8,128)(2,1)}, u32[]{:S(2)}, u32[]{:S(2)}) collective-permute-start(bf16[128,4096]{1,0:T(8,128)(2,1)S(1)} %collective-permute-done.refs_1_), channel_id=1, source_target_pairs={{0,31},{1,0},{2,1},{3,2},{4,3},{5,4},{6,5},{7,6},{8,7},{9,8},{10,9... | collective-permute-start | bytes 3145736 | tf_op jit(solution)/shard_map/ppermute | solution.py:33
  24.3 1.9 %collective-permute-start.3 = (bf16[128,4096]{1,0:T(8,128)(2,1)S(1)}, bf16[128,4096]{1,0:T(8,128)(2,1)}, u32[]{:S(2)}, u32[]{:S(2)}) collective-permute-start(bf16[128,4096]{1,0:T(8,128)(2,1)S(1)} %collective-permute-done.refs_1_), channel_id=1, source_target_pairs={{0,1},{1,2},{2,3},{3,4},{4,5},{5,6},{6,7},{7,8},{8,9},{9,10},{10,1... | collective-permute-start | bytes 3145736 | tf_op jit(solution)/shard_map/ppermute | solution.py:33
  26.3 4.9 %collective-permute-done.1.refs_2_ = bf16[128,4096]{1,0:T(8,128)(2,1)S(1)} collective-permute-done((bf16[128,4096]{1,0:T(8,128)(2,1)S(1)}, bf16[128,4096]{1,0:T(8,128)(2,1)S(1)}, u32[]{:S(2)}, u32[]{:S(2)}) %collective-permute-start.1) | collective-permute-done | bytes 1048608 | tf_op jit(solution)/shard_map/ppermute | solution.py:33
  31.2 1.9 %collective-permute-start.8 = (bf16[128,4096]{1,0:T(8,128)(2,1)S(1)}, bf16[128,4096]{1,0:T(8,128)(2,1)}, u32[]{:S(2)}, u32[]{:S(2)}) collective-permute-start(bf16[128,4096]{1,0:T(8,128)(2,1)S(1)} %collective-permute-done.1.refs_2_), channel_id=1, source_target_pairs={{0,96},{1,97},{2,98},{3,99},{4,100},{5,101},{6,102},{7,103},{8,104... | collective-permute-start | bytes 3145736 | tf_op jit(solution)/shard_map/ppermute | solution.py:33
  33.3 0.1 stack.64
  33.4 0.2 select_reduce_fusion
  33.5 0.1 concatenate.3.slots_ref
  33.6 10.3 %collective-permute-done.2.refs_3_ = bf16[128,4096]{1,0:T(8,128)(2,1)} collective-permute-done((bf16[128,4096]{1,0:T(8,128)(2,1)S(1)}, bf16[128,4096]{1,0:T(8,128)(2,1)}, u32[]{:S(2)}, u32[]{:S(2)}) %collective-permute-start.2) | collective-permute-done | bytes 1048608 | tf_op jit(solution)/shard_map/ppermute | solution.py:33
  44.0 2.8 %collective-permute-done.4.refs_5_ = bf16[128,4096]{1,0:T(8,128)(2,1)} collective-permute-done((bf16[128,4096]{1,0:T(8,128)(2,1)S(1)}, bf16[128,4096]{1,0:T(8,128)(2,1)}, u32[]{:S(2)}, u32[]{:S(2)}) %collective-permute-start.4) | collective-permute-done | bytes 1048608 | tf_op jit(solution)/shard_map/ppermute | solution.py:33
  46.8 0.7 collective-permute-start.5
  47.5 3.5 %collective-permute-start.6 = (bf16[128,4096]{1,0:T(8,128)(2,1)}, bf16[128,4096]{1,0:T(8,128)(2,1)S(1)}, u32[]{:S(2)}, u32[]{:S(2)}) collective-permute-start(bf16[128,4096]{1,0:T(8,128)(2,1)} %collective-permute-done.2.refs_3_), channel_id=1, source_target_pairs={{32,63},{33,32},{34,33},{35,34},{36,35},{37,36},{38,37},{39,38},{4... | collective-permute-start | bytes 3145736 | tf_op jit(solution)/shard_map/ppermute | solution.py:33
  51.0 2.4 %collective-permute-done.3.refs_4_ = bf16[128,4096]{1,0:T(8,128)(2,1)} collective-permute-done((bf16[128,4096]{1,0:T(8,128)(2,1)S(1)}, bf16[128,4096]{1,0:T(8,128)(2,1)}, u32[]{:S(2)}, u32[]{:S(2)}) %collective-permute-start.3) | collective-permute-done | bytes 1048608 | tf_op jit(solution)/shard_map/ppermute | solution.py:33
  53.5 3.7 %collective-permute-start.7 = (bf16[128,4096]{1,0:T(8,128)(2,1)}, bf16[128,4096]{1,0:T(8,128)(2,1)S(1)}, u32[]{:S(2)}, u32[]{:S(2)}) collective-permute-start(bf16[128,4096]{1,0:T(8,128)(2,1)} %collective-permute-done.3.refs_4_), channel_id=1, source_target_pairs={{0,1},{1,2},{2,3},{3,4},{4,5},{5,6},{6,7},{7,8},{8,9},{9,10},{10,1... | collective-permute-start | bytes 3145736 | tf_op jit(solution)/shard_map/ppermute | solution.py:33
  57.2 3.4 %near.1 = (f32[8,128]{1,0:T(8,128)S(1)}, f32[8,128]{1,0:T(8,128)S(1)}, f32[8,128]{1,0:T(8,128)S(1)}) custom-call(s32[1]{0:T(128)} %bitcast.11.flags_ref, s32[18]{0:T(128)S(1)} %concatenate.3.slots_ref, bf16[128,4096]{1,0:T(8,128)(2,1)S(1)} %get-tuple-element.14.refs_0_, bf16[128,4096]{1,0:T(8,128)(2,1)S(1)} %collective-permute-done.refs_1_, ...), custom_call_target="tpu_custom_call" | custom-call | flops 8053063680 | bytes 52428800 | tf_op jit(solution)/shard_map/near/pallas_call | solution.py:178
  60.6 4.4 %collective-permute-done.8.refs_9_ = bf16[128,4096]{1,0:T(8,128)(2,1)} collective-permute-done((bf16[128,4096]{1,0:T(8,128)(2,1)S(1)}, bf16[128,4096]{1,0:T(8,128)(2,1)}, u32[]{:S(2)}, u32[]{:S(2)}) %collective-permute-start.8) | collective-permute-done | bytes 1048608 | tf_op jit(solution)/shard_map/ppermute | solution.py:33
  65.0 3.4 %collective-permute-start.10 = (f32[8,128]{1,0:T(8,128)S(1)}, f32[8,128]{1,0:T(8,128)S(1)}, u32[]{:S(2)}, u32[]{:S(2)}) collective-permute-start(f32[8,128]{1,0:T(8,128)S(1)} %get-tuple-element.23), channel_id=1, source_target_pairs={{0,1},{1,2},{2,3},{3,4},{4,5},{5,6},{6,7},{7,8},{8,9},{9,10},{10,1... | collective-permute-start | bytes 12296 | tf_op jit(solution)/shard_map/ppermute | solution.py:33
  68.4 1.9 %collective-permute-start.9 = (f32[8,128]{1,0:T(8,128)S(1)}, f32[8,128]{1,0:T(8,128)S(1)}, u32[]{:S(2)}, u32[]{:S(2)}) collective-permute-start(f32[8,128]{1,0:T(8,128)S(1)} %get-tuple-element.22), channel_id=1, source_target_pairs={{0,31},{1,0},{2,1},{3,2},{4,3},{5,4},{6,5},{7,6},{8,7},{9,8},{10,9... | collective-permute-start | bytes 12296 | tf_op jit(solution)/shard_map/ppermute | solution.py:33
  70.3 4.9 %collective-permute-done.9 = f32[8,128]{1,0:T(8,128)S(1)} collective-permute-done((f32[8,128]{1,0:T(8,128)S(1)}, f32[8,128]{1,0:T(8,128)S(1)}, u32[]{:S(2)}, u32[]{:S(2)}) %collective-permute-start.9) | collective-permute-done | bytes 4128 | tf_op jit(solution)/shard_map/ppermute | solution.py:33
  75.3 4.0 %far.1 = f32[16,128]{1,0:T(8,128)S(1)} custom-call(s32[1]{0:T(128)} %bitcast.11.flags_ref, s32[18]{0:T(128)S(1)} %concatenate.3.slots_ref, bf16[128,4096]{1,0:T(8,128)(2,1)S(1)} %get-tuple-element.14.refs_0_, bf16[128,4096]{1,0:T(8,128)(2,1)S(1)} %collective-permute-done.refs_1_, bf16[128,4096]{1,0:T(8,128)(2,1)S(1)} %collective-permute-done.1.refs_2_, ...), custom_call_target="tpu_custom_call" | custom-call | flops 1073741824 | bytes 6291456 | tf_op jit(solution)/shard_map/far/pallas_call | solution.py:178
  79.3 0.1 select_select_fusion
  79.4 11.9 %all-gather = f32[64,128]{1,0:T(8,128)S(1)} all-gather(f32[16,128]{1,0:T(8,128)S(1)} %select_select_fusion), channel_id=2, replica_groups={{0,32,64,96},{128,160,192,224},{256,288,320,352},{384,416,448,480},{1,3..., dimensions={0}, use_global_device_ids=true | all-gather | bytes 40960 | tf_op jit(solution)/shard_map/all_gather | solution.py:42
  91.3 1.9 %collective-permute-start.11 = (f32[4,16,128]{2,1,0:T(8,128)S(1)}, f32[4,16,128]{2,1,0:T(8,128)S(1)}, u32[]{:S(2)}, u32[]{:S(2)}) collective-permute-start(f32[4,16,128]{2,1,0:T(8,128)S(1)} %bitcast.28), channel_id=1, source_target_pairs={{0,1},{1,2},{2,3},{3,4},{4,5},{5,6},{6,7},{7,8},{8,9},{9,10},{10,1... | collective-permute-start | bytes 98312 | tf_op jit(solution)/shard_map/ppermute | solution.py:33
  93.2 6.4 %collective-permute-start.12 = (f32[4,16,128]{2,1,0:T(8,128)S(1)}, f32[4,16,128]{2,1,0:T(8,128)S(1)}, u32[]{:S(2)}, u32[]{:S(2)}) collective-permute-start(f32[4,16,128]{2,1,0:T(8,128)S(1)} %bitcast.29), channel_id=1, source_target_pairs={{0,31},{1,0},{2,1},{3,2},{4,3},{5,4},{6,5},{7,6},{8,7},{9,8},{10,9... | collective-permute-start | bytes 98312 | tf_op jit(solution)/shard_map/ppermute | solution.py:33
  99.6 1.1 %collective-permute-done.12.backward_ref = f32[4,16,128]{2,1,0:T(8,128)S(1)} collective-permute-done((f32[4,16,128]{2,1,0:T(8,128)S(1)}, f32[4,16,128]{2,1,0:T(8,128)S(1)}, u32[]{:S(2)}, u32[]{:S(2)}) %collective-permute-start.12) | collective-permute-done | bytes 32800 | tf_op jit(solution)/shard_map/ppermute | solution.py:33
  100.7 0.6 copy-done.4
  101.3 1.4 %finish.1 = (f32[1,2]{1,0:T(1,128)}, f32[2,1,128]{2,1,0:T(1,128)}) custom-call(s32[18]{0:T(128)} %copy-done.1, f32[4,16,128]{2,1,0:T(8,128)} %bitcast.30, f32[4,16,128]{2,1,0:T(8,128)} %copy-done.3, f32[4,16,128]{2,1,0:T(8,128)} %copy-done.4), custom_call_target="tpu_custom_call" | custom-call | tf_op jit(solution)/shard_map/finish/pallas_call | solution.py:268
  (18 shorter events, 0.0 us)
Async XLA Ops:
  0.6 32.6 %copy-start.5 = (s32[2,512]{1,0:T(2,128)S(1)}, s32[2,512]{1,0:T(2,128)}, u32[]{:S(2)}) copy-start(s32[2,512]{1,0:T(2,128)} %param.3) | copy-start | bytes 12292
  0.7 1.6 %copy-start = (bf16[2,1,128,4096]{3,2,1,0:T(8,128)(2,1)S(1)}, bf16[2,1,128,4096]{3,2,1,0:T(8,128)(2,1)}, u32[]{:S(2)}) copy-start(bf16[2,1,128,4096]{3,2,1,0:T(8,128)(2,1)} %param.2) | copy-start | bytes 6291460
  3.5 17.4 %collective-permute-start = (bf16[128,4096]{1,0:T(8,128)(2,1)S(1)}, bf16[128,4096]{1,0:T(8,128)(2,1)S(1)}, u32[]{:S(2)}, u32[]{:S(2)}) collective-permute-start(bf16[128,4096]{1,0:T(8,128)(2,1)S(1)} %get-tuple-element.15), channel_id=1, source_target_pairs={{0,32},{1,33},{2,34},{3,35},{4,36},{5,37},{6,38},{7,39},{8,40},{9,... | collective-permute-start | bytes 3145736 | tf_op jit(solution)/shard_map/ppermute | solution.py:33
  12.3 18.9 %collective-permute-start.1 = (bf16[128,4096]{1,0:T(8,128)(2,1)S(1)}, bf16[128,4096]{1,0:T(8,128)(2,1)S(1)}, u32[]{:S(2)}, u32[]{:S(2)}) collective-permute-start(bf16[128,4096]{1,0:T(8,128)(2,1)S(1)} %get-tuple-element.14.refs_0_), channel_id=1, source_target_pairs={{0,31},{1,0},{2,1},{3,2},{4,3},{5,4},{6,5},{7,6},{8,7},{9,8},{10,9... | collective-permute-start | bytes 3145736 | tf_op jit(solution)/shard_map/ppermute | solution.py:33
  14.3 29.7 %collective-permute-start.2 = (bf16[128,4096]{1,0:T(8,128)(2,1)S(1)}, bf16[128,4096]{1,0:T(8,128)(2,1)}, u32[]{:S(2)}, u32[]{:S(2)}) collective-permute-start(bf16[128,4096]{1,0:T(8,128)(2,1)S(1)} %get-tuple-element.14.refs_0_), channel_id=1, source_target_pairs={{0,96},{1,97},{2,98},{3,99},{4,100},{5,101},{6,102},{7,103},{8,104... | collective-permute-start | bytes 3145736 | tf_op jit(solution)/shard_map/ppermute | solution.py:33
  21.0 25.8 %collective-permute-start.4 = (bf16[128,4096]{1,0:T(8,128)(2,1)S(1)}, bf16[128,4096]{1,0:T(8,128)(2,1)}, u32[]{:S(2)}, u32[]{:S(2)}) collective-permute-start(bf16[128,4096]{1,0:T(8,128)(2,1)S(1)} %collective-permute-done.refs_1_), channel_id=1, source_target_pairs={{0,31},{1,0},{2,1},{3,2},{4,3},{5,4},{6,5},{7,6},{8,7},{9,8},{10,9... | collective-permute-start | bytes 3145736 | tf_op jit(solution)/shard_map/ppermute | solution.py:33
  24.3 29.1 %collective-permute-start.3 = (bf16[128,4096]{1,0:T(8,128)(2,1)S(1)}, bf16[128,4096]{1,0:T(8,128)(2,1)}, u32[]{:S(2)}, u32[]{:S(2)}) collective-permute-start(bf16[128,4096]{1,0:T(8,128)(2,1)S(1)} %collective-permute-done.refs_1_), channel_id=1, source_target_pairs={{0,1},{1,2},{2,3},{3,4},{4,5},{5,6},{6,7},{7,8},{8,9},{9,10},{10,1... | collective-permute-start | bytes 3145736 | tf_op jit(solution)/shard_map/ppermute | solution.py:33
  31.2 33.8 %collective-permute-start.8 = (bf16[128,4096]{1,0:T(8,128)(2,1)S(1)}, bf16[128,4096]{1,0:T(8,128)(2,1)}, u32[]{:S(2)}, u32[]{:S(2)}) collective-permute-start(bf16[128,4096]{1,0:T(8,128)(2,1)S(1)} %collective-permute-done.1.refs_2_), channel_id=1, source_target_pairs={{0,96},{1,97},{2,98},{3,99},{4,100},{5,101},{6,102},{7,103},{8,104... | collective-permute-start | bytes 3145736 | tf_op jit(solution)/shard_map/ppermute | solution.py:33
  33.6 41.6 %copy-start.1 = (s32[18]{0:T(128)}, s32[18]{0:T(128)S(1)}, u32[]{:S(2)}) copy-start(s32[18]{0:T(128)S(1)} %concatenate.3.slots_ref) | copy-start | bytes 220
  46.8 28.5 %collective-permute-start.5 = (bf16[128,4096]{1,0:T(8,128)(2,1)}, bf16[128,4096]{1,0:T(8,128)(2,1)S(1)}, u32[]{:S(2)}, u32[]{:S(2)}) collective-permute-start(bf16[128,4096]{1,0:T(8,128)(2,1)} %collective-permute-done.4.refs_5_), channel_id=1, source_target_pairs={{0,31},{1,0},{2,1},{3,2},{4,3},{5,4},{6,5},{7,6},{8,7},{9,8},{10,9... | collective-permute-start | bytes 3145736 | tf_op jit(solution)/shard_map/ppermute | solution.py:33
  47.5 27.7 %collective-permute-start.6 = (bf16[128,4096]{1,0:T(8,128)(2,1)}, bf16[128,4096]{1,0:T(8,128)(2,1)S(1)}, u32[]{:S(2)}, u32[]{:S(2)}) collective-permute-start(bf16[128,4096]{1,0:T(8,128)(2,1)} %collective-permute-done.2.refs_3_), channel_id=1, source_target_pairs={{32,63},{33,32},{34,33},{35,34},{36,35},{37,36},{38,37},{39,38},{4... | collective-permute-start | bytes 3145736 | tf_op jit(solution)/shard_map/ppermute | solution.py:33
  53.5 21.8 %collective-permute-start.7 = (bf16[128,4096]{1,0:T(8,128)(2,1)}, bf16[128,4096]{1,0:T(8,128)(2,1)S(1)}, u32[]{:S(2)}, u32[]{:S(2)}) collective-permute-start(bf16[128,4096]{1,0:T(8,128)(2,1)} %collective-permute-done.3.refs_4_), channel_id=1, source_target_pairs={{0,1},{1,2},{2,3},{3,4},{4,5},{5,6},{6,7},{7,8},{8,9},{9,10},{10,1... | collective-permute-start | bytes 3145736 | tf_op jit(solution)/shard_map/ppermute | solution.py:33
  65.0 5.3 %collective-permute-start.10 = (f32[8,128]{1,0:T(8,128)S(1)}, f32[8,128]{1,0:T(8,128)S(1)}, u32[]{:S(2)}, u32[]{:S(2)}) collective-permute-start(f32[8,128]{1,0:T(8,128)S(1)} %get-tuple-element.23), channel_id=1, source_target_pairs={{0,1},{1,2},{2,3},{3,4},{4,5},{5,6},{6,7},{7,8},{8,9},{9,10},{10,1... | collective-permute-start | bytes 12296 | tf_op jit(solution)/shard_map/ppermute | solution.py:33
  68.4 6.9 %collective-permute-start.9 = (f32[8,128]{1,0:T(8,128)S(1)}, f32[8,128]{1,0:T(8,128)S(1)}, u32[]{:S(2)}, u32[]{:S(2)}) collective-permute-start(f32[8,128]{1,0:T(8,128)S(1)} %get-tuple-element.22), channel_id=1, source_target_pairs={{0,31},{1,0},{2,1},{3,2},{4,3},{5,4},{6,5},{7,6},{8,7},{9,8},{10,9... | collective-permute-start | bytes 12296 | tf_op jit(solution)/shard_map/ppermute | solution.py:33
  91.3 9.5 %copy-start.2 = (f32[64,128]{1,0:T(8,128)}, f32[64,128]{1,0:T(8,128)S(1)}, u32[]{:S(2)}) copy-start(f32[64,128]{1,0:T(8,128)S(1)} %all-gather) | copy-start | bytes 98308
  91.3 8.3 %collective-permute-start.11 = (f32[4,16,128]{2,1,0:T(8,128)S(1)}, f32[4,16,128]{2,1,0:T(8,128)S(1)}, u32[]{:S(2)}, u32[]{:S(2)}) collective-permute-start(f32[4,16,128]{2,1,0:T(8,128)S(1)} %bitcast.28), channel_id=1, source_target_pairs={{0,1},{1,2},{2,3},{3,4},{4,5},{5,6},{6,7},{7,8},{8,9},{9,10},{10,1... | collective-permute-start | bytes 98312 | tf_op jit(solution)/shard_map/ppermute | solution.py:33
  93.2 7.5 %collective-permute-start.12 = (f32[4,16,128]{2,1,0:T(8,128)S(1)}, f32[4,16,128]{2,1,0:T(8,128)S(1)}, u32[]{:S(2)}, u32[]{:S(2)}) collective-permute-start(f32[4,16,128]{2,1,0:T(8,128)S(1)} %bitcast.29), channel_id=1, source_target_pairs={{0,31},{1,0},{2,1},{3,2},{4,3},{5,4},{6,5},{7,6},{8,7},{9,8},{10,9... | collective-permute-start | bytes 98312 | tf_op jit(solution)/shard_map/ppermute | solution.py:33
  99.6 1.1 %copy-start.3 = (f32[4,16,128]{2,1,0:T(8,128)}, f32[4,16,128]{2,1,0:T(8,128)S(1)}, u32[]{:S(2)}) copy-start(f32[4,16,128]{2,1,0:T(8,128)S(1)} %collective-permute-done.11.onward_ref) | copy-start | bytes 98308
  100.7 0.6 copy-start.4
